TPU v7x, 32 devices: a whole 2x2x4 slice. The times are simulated.
32 devices in a mesh: fsdp: 4 (over y, x), ctx: 8 (over z, core).
Axes of the slice: x: 2, y: 2, z: 4, core: 2. Of those that a mesh axis runs over, the one named last changes fastest.
Arguments:
- tokens: bfloat16 [4, 1024, 1600], P('fsdp', 'ctx'), may hold values from -6 to 6
- block_order: int32 [16], replicated, may hold values from 0 to 15, each once
- cotangent: bfloat16 [4, 1024, 1600], P('fsdp', 'ctx'), may hold values from -6 to 6
- pre_attn_gain: bfloat16 [1600], P('ctx'), may hold values from 0.5 to 1.5
- pre_attn_bias: bfloat16 [1600], P('ctx'), may hold values from -1.25 to 1.25
- qkv_weight: bfloat16 [1600, 4800], P('fsdp', 'ctx'), may hold values from -0.21875 to 0.21875
- query_bias: bfloat16 [1600], P('ctx'), may hold values from -1.75 to 1.75
- value_bias: bfloat16 [1600], P('ctx'), may hold values from -1.75 to 1.75
- out_weight: bfloat16 [1600, 1600], P('fsdp', 'ctx'), may hold values from -0.875 to 0.875
- out_bias: bfloat16 [1600], P('ctx'), may hold values from -1.75 to 1.75
- pre_mlp_gain: bfloat16 [1600], P('ctx'), may hold values from 0.5 to 1.5
- pre_mlp_bias: bfloat16 [1600], P('ctx'), may hold values from -1.25 to 1.25
- fc_weight: bfloat16 [1600, 6400], P('fsdp', 'ctx'), may hold values from -0.15625 to 0.15625
- fc_bias: bfloat16 [6400], P('ctx'), may hold values from -1.75 to 1.75
- proj_weight: bfloat16 [6400, 1600], P('fsdp', 'ctx'), may hold values from -0.15625 to 0.15625
- proj_bias: bfloat16 [1600], P('ctx'), may hold values from -1.75 to 1.75
Outputs:
- output: bfloat16 [4, 1024, 1600], P('fsdp', 'ctx')
- input_grad: float32 [4, 1024, 1600], P('fsdp', 'ctx')
- pre_attn_gain_grad: float32 [1600], P('ctx')
- pre_attn_bias_grad: float32 [1600], P('ctx')
- qkv_weight_grad: float32 [1600, 4800], P('fsdp', 'ctx')
- query_bias_grad: float32 [1600], P('ctx')
- value_bias_grad: float32 [1600], P('ctx')
- out_weight_grad: float32 [1600, 1600], P('fsdp', 'ctx')
- out_bias_grad: float32 [1600], P('ctx')
- pre_mlp_gain_grad: float32 [1600], P('ctx')
- pre_mlp_bias_grad: float32 [1600], P('ctx')
- fc_weight_grad: float32 [1600, 6400], P('fsdp', 'ctx')
- fc_bias_grad: float32 [6400], P('ctx')
- proj_weight_grad: float32 [6400, 1600], P('fsdp', 'ctx')
- proj_bias_grad: float32 [1600], P('ctx')
Inputs may be any that keep to these rules, and one draw needn't show every extreme that they name: `block_order`: each stored block holds one position block; every value appears once.
All inputs are finite; a program needn't handle non-finite values.
Results may differ from a plain program's by a relative error of at most 0.022.
Values may be sent and summed in bfloat16 or wider, within the bound.
A program may use at most 320 MiB of HBM per device.

v0:
```python
from functools import partial

import jax
import jax.numpy as jnp
from jax import lax
from jax.sharding import PartitionSpec as P

D = 1600
H = 25
HD = 64


epsilon = 1e-05
floor_score = -1e30


def positions(order_table, first_row, row_count, block_rows):
    stored = first_row + jnp.arange(row_count, dtype=jnp.int32)
    slot_now = stored // block_rows
    slot_ids = jnp.arange(order_table.shape[0], dtype=jnp.int32)
    picked = jnp.sum(
        jnp.where(slot_now[:, None] == slot_ids[None, :], order_table[None, :], 0), axis=1
    )
    return picked * block_rows + stored % block_rows


def apply_layer_norm(input_rows, gain, shift):
    centred = input_rows - jnp.mean(input_rows, axis=-1, keepdims=True)
    scaled = lax.rsqrt(jnp.mean(centred * centred, axis=-1, keepdims=True) + epsilon)
    normed = centred * scaled
    return (normed * gain + shift, normed, scaled)


def layer_norm_backward(upstream, normed, scaled, gain):
    inner = upstream * gain
    return scaled * (
        inner
        - jnp.mean(inner, axis=-1, keepdims=True)
        - normed * jnp.mean(inner * normed, axis=-1, keepdims=True)
    )


def add_small(stacked, hidden_part):
    return (
        lax.psum(stacked.astype(jnp.bfloat16), "fsdp").astype(jnp.float32),
        lax.psum(hidden_part.astype(jnp.bfloat16), "fsdp").astype(jnp.float32),
    )


def grad_scores(
    query_heads,
    grad_heads,
    log_rows,
    delta_vals,
    query_places,
    key_rows,
    value_rows,
    key_places,
    scale,
):
    scores = (
        jnp.einsum("qhd,khd->hqk", query_heads, key_rows, preferred_element_type=jnp.float32)
        * scale
    )
    allowed = key_places[None, None, :] <= query_places[None, :, None]
    probs = jnp.where(allowed, jnp.exp(scores - log_rows[:, :, None]), 0.0)
    d_probs = jnp.einsum("qhd,khd->hqk", grad_heads, value_rows, preferred_element_type=jnp.float32)
    d_scores = (probs * (d_probs - delta_vals[:, :, None])).astype(jnp.bfloat16)
    return (probs, d_scores)


def body(
    tokens,
    block_order,
    cotangent,
    pre_attn_gain,
    pre_attn_bias,
    qkv_weight,
    query_bias,
    value_bias,
    out_weight,
    out_bias,
    pre_mlp_gain,
    pre_mlp_bias,
    fc_weight,
    fc_bias,
    proj_weight,
    proj_bias,
):
    rows_local = tokens.shape[1]
    half_rows = rows_local // 2
    scale = HD ** (-0.5)
    cycle_size = lax.axis_size("ctx")
    qkv_rows, out_rows, fc_rows, proj_rows = (
        lax.all_gather(qkv_weight, "fsdp", axis=0, tiled=True),
        lax.all_gather(out_weight, "fsdp", axis=0, tiled=True),
        lax.all_gather(fc_weight, "fsdp", axis=0, tiled=True),
        lax.all_gather(proj_weight, "fsdp", axis=0, tiled=True),
    )
    gathered = (
        lax.all_gather(qkv_rows, "ctx", axis=1, tiled=True),
        lax.all_gather(out_rows, "ctx", axis=1, tiled=True),
        lax.all_gather(fc_rows, "ctx", axis=1, tiled=True),
        lax.all_gather(proj_rows, "ctx", axis=1, tiled=True),
        lax.all_gather(pre_attn_gain[None, :], "ctx", axis=1, tiled=True),
        lax.all_gather(pre_attn_bias[None, :], "ctx", axis=1, tiled=True),
        lax.all_gather(query_bias[None, :], "ctx", axis=1, tiled=True),
        lax.all_gather(value_bias[None, :], "ctx", axis=1, tiled=True),
        lax.all_gather(out_bias[None, :], "ctx", axis=1, tiled=True),
        lax.all_gather(pre_mlp_gain[None, :], "ctx", axis=1, tiled=True),
        lax.all_gather(pre_mlp_bias[None, :], "ctx", axis=1, tiled=True),
        lax.all_gather(fc_bias[None, :], "ctx", axis=1, tiled=True),
        lax.all_gather(proj_bias[None, :], "ctx", axis=1, tiled=True),
    )
    qkv_full, out_full, fc_full, proj_full = (gathered[0], gathered[1], gathered[2], gathered[3])
    (
        attention_gain_vector,
        attention_shift_vector,
        query_shift,
        value_shift,
        output_shift,
        feedforward_gain,
        feedforward_shift,
        fc_shift,
        proj_shift,
    ) = [entry[0].astype(jnp.float32) for entry in gathered[4:]]
    input_rows = tokens[0].astype(jnp.float32)
    first_normed_rows, first_centred_scaled, first_inverse_deviation = apply_layer_norm(
        input_rows, attention_gain_vector, attention_shift_vector
    )
    hidden_one = first_normed_rows.astype(jnp.bfloat16)
    shift_row = jnp.concatenate([query_shift, jnp.zeros((D,), jnp.float32), value_shift])
    projected = (
        jnp.dot(hidden_one, qkv_full, preferred_element_type=jnp.float32) + shift_row
    ).astype(jnp.bfloat16)
    queries = projected[:, :D].reshape(rows_local, H, HD)
    key_value = projected[:, D:]
    query_pos = positions(block_order, lax.axis_index("ctx") * rows_local, rows_local, half_rows)

    def attend(state_now, key_block, first_row):
        top_now, sum_now, acc_now = state_now
        key_pos = positions(block_order, first_row, rows_local, half_rows)
        key_rows = key_block[:, :D].reshape(rows_local, H, HD)
        value_rows = key_block[:, D:].reshape(rows_local, H, HD)
        scores = (
            jnp.einsum("qhd,khd->hqk", queries, key_rows, preferred_element_type=jnp.float32)
            * scale
        )
        allowed = key_pos[None, None, :] <= query_pos[None, :, None]
        top_new = jnp.maximum(top_now, jnp.max(jnp.where(allowed, scores, floor_score), axis=2))
        weights = jnp.where(allowed, jnp.exp(scores - top_new[:, :, None]), 0.0)
        shrink = jnp.exp(top_now - top_new)
        sum_new = sum_now * shrink + jnp.sum(weights, axis=2)
        acc_new = acc_now * jnp.transpose(shrink)[:, :, None] + jnp.einsum(
            "hqk,khd->qhd",
            weights.astype(jnp.bfloat16),
            value_rows,
            preferred_element_type=jnp.float32,
        )
        return (top_new, sum_new, acc_new)

    start_state = (
        jnp.full((H, rows_local), floor_score, jnp.float32),
        jnp.zeros((H, rows_local), jnp.float32),
        jnp.zeros((rows_local, H, HD), jnp.float32),
    )
    shard_rows = lax.all_gather(key_value, "ctx", axis=0, tiled=True)

    def one_block(index, inner):
        block_now = lax.dynamic_slice_in_dim(shard_rows, index * rows_local, rows_local, 0)
        return attend(inner, block_now, index * rows_local)

    top_end, sum_end, acc_end = lax.fori_loop(
        0, shard_rows.shape[0] // rows_local, one_block, start_state
    )
    attended_full = acc_end / jnp.transpose(sum_end)[:, :, None]
    log_total = top_end + jnp.log(sum_end)
    attended = attended_full.reshape(rows_local, D).astype(jnp.bfloat16)
    middle_rows = (
        input_rows + jnp.dot(attended, out_full, preferred_element_type=jnp.float32) + output_shift
    )
    second_normed_rows, second_centred_scaled, second_inverse_deviation = apply_layer_norm(
        middle_rows, feedforward_gain, feedforward_shift
    )
    hidden_two = second_normed_rows.astype(jnp.bfloat16)
    before = jnp.dot(hidden_two, fc_full, preferred_element_type=jnp.float32) + fc_shift
    activated = jax.nn.gelu(before, approximate=True).astype(jnp.bfloat16)
    output = (
        middle_rows + jnp.dot(activated, proj_full, preferred_element_type=jnp.float32) + proj_shift
    ).astype(jnp.bfloat16)
    upstream = cotangent[0]
    upstream_gradient_whole = upstream.astype(jnp.float32)
    d_activated = jnp.einsum("td,fd->tf", upstream, proj_full, preferred_element_type=jnp.float32)
    gelu_back = jax.vjp(partial(jax.nn.gelu, approximate=True), before)[1]
    d_before = gelu_back(d_activated)[0].astype(jnp.bfloat16)
    second_hidden_gradient = jnp.einsum(
        "tf,df->td", d_before, fc_full, preferred_element_type=jnp.float32
    )
    middle_gradient_rows = upstream_gradient_whole + layer_norm_backward(
        second_hidden_gradient, second_centred_scaled, second_inverse_deviation, feedforward_gain
    )
    d_branch = middle_gradient_rows.astype(jnp.bfloat16)
    d_attended = jnp.einsum(
        "te,de->td", d_branch, out_full, preferred_element_type=jnp.float32
    ).astype(jnp.bfloat16)
    d_heads = d_attended.reshape(rows_local, H, HD)
    delta_rows = jnp.einsum("qhd,qhd->hq", d_heads.astype(jnp.float32), attended_full)

    def back_block(state_now, key_block, first_row):
        d_query_now, d_kv_now = state_now
        key_pos = positions(block_order, first_row, rows_local, half_rows)
        key_rows = key_block[:, :D].reshape(rows_local, H, HD)
        value_rows = key_block[:, D:].reshape(rows_local, H, HD)
        probs, d_scores = grad_scores(
            queries, d_heads, log_total, delta_rows, query_pos, key_rows, value_rows, key_pos, scale
        )
        d_query_new = d_query_now + jnp.einsum(
            "hqk,khd->qhd", d_scores, key_rows, preferred_element_type=jnp.float32
        )
        d_keys = (
            jnp.einsum("hqk,qhd->khd", d_scores, queries, preferred_element_type=jnp.float32)
            * scale
        )
        d_values = jnp.einsum(
            "hqk,qhd->khd", probs.astype(jnp.bfloat16), d_heads, preferred_element_type=jnp.float32
        )
        block_grad = jnp.concatenate(
            [d_keys.reshape(rows_local, D), d_values.reshape(rows_local, D)], axis=1
        )
        return (d_query_new, lax.dynamic_update_slice_in_dim(d_kv_now, block_grad, first_row, 0))

    back_start = (
        jnp.zeros((rows_local, H, HD), jnp.float32),
        jnp.zeros((rows_local * cycle_size, 2 * D), jnp.float32),
    )
    fold_shard_rows = lax.all_gather(key_value, "ctx", axis=0, tiled=True)

    def one_block(index, inner):
        block_now = lax.dynamic_slice_in_dim(fold_shard_rows, index * rows_local, rows_local, 0)
        return back_block(inner, block_now, index * rows_local)

    back_end = lax.fori_loop(0, fold_shard_rows.shape[0] // rows_local, one_block, back_start)
    d_query_end, d_kv_end = back_end
    key_grad_sum = lax.psum_scatter(
        d_kv_end.astype(jnp.bfloat16), "ctx", scatter_dimension=0, tiled=True
    )
    d_query_low = (d_query_end * scale).reshape(rows_local, D).astype(jnp.bfloat16)
    d_projected = jnp.concatenate([d_query_low, key_grad_sum], axis=1)
    first_hidden_gradient = jnp.einsum(
        "te,de->td", d_projected, qkv_full, preferred_element_type=jnp.float32
    )
    input_gradient_rows = middle_gradient_rows + layer_norm_backward(
        first_hidden_gradient, first_centred_scaled, first_inverse_deviation, attention_gain_vector
    )
    small_stack = jnp.stack(
        [
            jnp.sum(first_hidden_gradient * first_centred_scaled, axis=0),
            jnp.sum(first_hidden_gradient, axis=0),
            jnp.sum(d_query_low.astype(jnp.float32), axis=0),
            jnp.sum(key_grad_sum[:, D:].astype(jnp.float32), axis=0),
            jnp.sum(d_branch.astype(jnp.float32), axis=0),
            jnp.sum(second_hidden_gradient * second_centred_scaled, axis=0),
            jnp.sum(second_hidden_gradient, axis=0),
            jnp.sum(upstream_gradient_whole, axis=0),
        ],
        axis=0,
    )
    hidden_small = jnp.sum(d_before.astype(jnp.float32), axis=0)[None, :]
    column_parts = (
        lax.psum_scatter(
            jnp.einsum(
                "td,te->de", hidden_one, d_projected, preferred_element_type=jnp.float32
            ).astype(jnp.bfloat16),
            "ctx",
            scatter_dimension=1,
            tiled=True,
        ).astype(jnp.float32),
        lax.psum_scatter(
            jnp.einsum("td,te->de", attended, d_branch, preferred_element_type=jnp.float32).astype(
                jnp.bfloat16
            ),
            "ctx",
            scatter_dimension=1,
            tiled=True,
        ).astype(jnp.float32),
        lax.psum_scatter(
            jnp.einsum(
                "td,te->de", hidden_two, d_before, preferred_element_type=jnp.float32
            ).astype(jnp.bfloat16),
            "ctx",
            scatter_dimension=1,
            tiled=True,
        ).astype(jnp.float32),
        lax.psum_scatter(
            jnp.einsum("td,te->de", activated, upstream, preferred_element_type=jnp.float32).astype(
                jnp.bfloat16
            ),
            "ctx",
            scatter_dimension=1,
            tiled=True,
        ).astype(jnp.float32),
        lax.psum_scatter(
            small_stack.astype(jnp.bfloat16), "ctx", scatter_dimension=1, tiled=True
        ).astype(jnp.float32),
        lax.psum_scatter(
            hidden_small.astype(jnp.bfloat16), "ctx", scatter_dimension=1, tiled=True
        ).astype(jnp.float32),
    )
    qkv_grad, out_grad, fc_grad, proj_grad = (
        lax.psum_scatter(
            column_parts[0].astype(jnp.bfloat16), "fsdp", scatter_dimension=0, tiled=True
        ).astype(jnp.float32),
        lax.psum_scatter(
            column_parts[1].astype(jnp.bfloat16), "fsdp", scatter_dimension=0, tiled=True
        ).astype(jnp.float32),
        lax.psum_scatter(
            column_parts[2].astype(jnp.bfloat16), "fsdp", scatter_dimension=0, tiled=True
        ).astype(jnp.float32),
        lax.psum_scatter(
            column_parts[3].astype(jnp.bfloat16), "fsdp", scatter_dimension=0, tiled=True
        ).astype(jnp.float32),
    )
    stack_grad, hidden_grad = add_small(column_parts[4], column_parts[5])
    return (
        output[None],
        input_gradient_rows[None],
        stack_grad[0],
        stack_grad[1],
        qkv_grad,
        stack_grad[2],
        stack_grad[3],
        out_grad,
        stack_grad[4],
        stack_grad[5],
        stack_grad[6],
        fc_grad,
        hidden_grad[0],
        proj_grad,
        stack_grad[7],
    )


def solution(mesh):
    in_specs = (
        P("fsdp", "ctx", None),
        P(),
        P("fsdp", "ctx", None),
        P("ctx"),
        P("ctx"),
        P("fsdp", "ctx"),
        P("ctx"),
        P("ctx"),
        P("fsdp", "ctx"),
        P("ctx"),
        P("ctx"),
        P("ctx"),
        P("fsdp", "ctx"),
        P("ctx"),
        P("fsdp", "ctx"),
        P("ctx"),
    )
    out_specs = (
        P("fsdp", "ctx", None),
        P("fsdp", "ctx", None),
        P("ctx"),
        P("ctx"),
        P("fsdp", "ctx"),
        P("ctx"),
        P("ctx"),
        P("fsdp", "ctx"),
        P("ctx"),
        P("ctx"),
        P("ctx"),
        P("fsdp", "ctx"),
        P("ctx"),
        P("fsdp", "ctx"),
        P("ctx"),
    )
    return jax.shard_map(body, mesh=mesh, in_specs=in_specs, out_specs=out_specs, check_vma=False)
```

profile of v0, /device:TPU:0, one launch (start us, length us, event | category | flops | bytes accessed | tf_op | source)
XLA Modules:
  0.0 1823.5 jit_solution(3315357451684361123)
XLA Ops:
  8.1 39.4 %all-gather.19.cloned.1.call-done = bf16[1600,600]{1,0:T(8,128)(2,1)} async-done(((bf16[400,600]{1,0:T(8,128)(2,1)}), bf16[1600,600]{1,0:T(8,128)(2,1)}) %all-gather.19.cloned.1.call-update) | async-done | bytes 1920016 | tf_op jit(solution)/shard_map/all_gather | solution.py:95
  56.9 30.3 %all-reduce.16 = (bf16[1600]{0:T(1024)(128)(2,1)S(1)}, bf16[1600]{0:T(1024)(128)(2,1)S(1)}, bf16[1600]{0:T(1024)(128)(2,1)S(1)}, bf16[1600]{0:T(1024)(128)(2,1)S...) all-reduce(bf16[1600]{0:T(1024)(128)(2,1)S(1)} %dynamic-update-slic, ...), channel_id=4, replica_groups=mesh['fsdp'=4,'ctx'=8] {'ctx'}, use_global_device_ids=true, to_apply=%add.2 | all-reduce | flops 17600 | bytes 70400
  87.8 109.4 %all-gather.21.cloned.1.call-done = bf16[1600,4800]{0,1:T(8,128)(2,1)} async-done(((bf16[1600,600]{0,1:T(8,128)(2,1)}), bf16[1600,4800]{0,1:T(8,128)(2,1)}) %all-gather.21.cloned.1.call-update) | async-done | bytes 15360016 | tf_op jit(solution)/shard_map/all_gather | solution.py:101
  197.2 10.0 fusion.21
  209.3 15.1 all_gather.62
  225.7 15.9 all-gather.27.cloned.1.call-done
  247.1 36.3 %all-gather.33.cloned.1.call-done = bf16[4,1600,200]{1,2,0:T(8,128)(2,1)} async-done(((bf16[1,1600,200]{1,2,0:T(8,128)(2,1)}), bf16[4,1600,200]{1,2,0:T(8,128)(2,1)}) %all-gather.33.cloned.1.call-update) | async-done | bytes 2560016 | tf_op jit(solution)/shard_map/all_gather | solution.py:98
  290.9 61.8 %all-gather.23.cloned.1.call-done = bf16[1024,3200]{0,1:T(8,128)(2,1)} async-done(((bf16[128,3200]{0,1:T(8,128)(2,1)}), bf16[1024,3200]{0,1:T(8,128)(2,1)}) %all-gather.23.cloned.1.call-update) | async-done | bytes 6553616 | tf_op jit(solution)/shard_map/all_gather | solution.py:167
  352.7 22.8 %while.38 = (s32[]{:T(128)}, f32[25,128]{1,0:T(8,128)S(1)}, f32[25,128]{1,0:T(8,128)S(1)}, f32[128,25,64]{0,2,1:T(8,128)S(1)}, s32[16]{0:T(128)S(1)}, /*index=5*...) while((s32[]{:T(128)}, f32[25,128]{1,0:T(8,128)S(1)}, ...), condition=%wide.region_7.8_spmd.clone, body=%wide.region_3.7_spmd.clone.sunk | while | flops 110023048 | bytes 9695003 | solution.py:173
  376.4 33.4 %all-gather.25.cloned.1.call-done = bf16[1600,1600]{0,1:T(8,128)(2,1)} async-done(((bf16[1600,200]{0,1:T(8,128)(2,1)}), bf16[1600,1600]{0,1:T(8,128)(2,1)}) %all-gather.25.cloned.1.call-update) | async-done | bytes 5120016 | tf_op jit(solution)/shard_map/all_gather | solution.py:102
  414.2 184.2 %all-gather.29.cloned.1.call-done = bf16[1600,6400]{0,1:T(8,128)(2,1)} async-done(((bf16[1600,800]{0,1:T(8,128)(2,1)}), bf16[1600,6400]{0,1:T(8,128)(2,1)}) %all-gather.29.cloned.1.call-update) | async-done | bytes 20480016 | tf_op jit(solution)/shard_map/all_gather | solution.py:103
  598.3 13.0 convolution_add_fusion
  611.3 168.3 %all-gather.31.cloned.1.call-done = bf16[6400,1600]{0,1:T(8,128)(2,1)} async-done(((bf16[6400,200]{0,1:T(8,128)(2,1)}), bf16[6400,1600]{0,1:T(8,128)(2,1)}) %all-gather.31.cloned.1.call-update) | async-done | bytes 20480016 | tf_op jit(solution)/shard_map/all_gather | solution.py:104
  779.7 14.4 fusion.70
  794.1 15.8 multiply_reduce_fusion
  820.3 41.6 %while.39 = (s32[]{:T(128)}, f32[128,25,64]{0,2,1:T(8,128)S(1)}, bf16[1024,3200]{0,1:T(8,128)(2,1)}, bf16[1024,3200]{0,1:T(8,128)(2,1)}, s32[16]{0:T(128)S(1)}, ...) while((s32[]{:T(128)}, f32[128,25,64]{0,2,1:T(8,128)S(1)}, ...), condition=%wide.region_14.15_spmd.clone, body=%wide.region_12.14_spmd.clone.sunk | while | flops 267495040 | bytes 16036653 | solution.py:242
  861.9 9.2 copy.90
  877.4 11.8 convolution_convert_fusion
  889.2 11.4 convolution_convert_fusion.1
  901.9 39.9 %reduce-scatter.28.cloned.1.call-done = bf16[128,3200]{1,0:T(8,128)(2,1)} async-done(((bf16[1024,3200]{1,0:T(8,128)(2,1)}), bf16[128,3200]{1,0:T(8,128)(2,1)}) %reduce-scatter.28.cloned.1.call-update) | async-done | bytes 819216
  943.5 11.1 convolution_convert_fusion.2
  958.7 44.8 %reduce-scatter.38.cloned.1.call-done = bf16[1600,200]{0,1:T(8,128)(2,1)} async-done(((bf16[1600,1600]{0,1:T(8,128)(2,1)}), bf16[1600,200]{0,1:T(8,128)(2,1)}) %reduce-scatter.38.cloned.1.call-update) | async-done | bytes 640016
  1005.9 203.0 %reduce-scatter.40.cloned.1.call-done = bf16[6400,200]{0,1:T(8,128)(2,1)} async-done(((bf16[6400,1600]{0,1:T(8,128)(2,1)}), bf16[6400,200]{0,1:T(8,128)(2,1)}) %reduce-scatter.40.cloned.1.call-update) | async-done | bytes 2560016
  1213.9 206.9 %reduce-scatter.26.cloned.1.call-done = bf16[1600,800]{0,1:T(8,128)(2,1)} async-done(((bf16[1600,6400]{0,1:T(8,128)(2,1)}), bf16[1600,800]{0,1:T(8,128)(2,1)}) %reduce-scatter.26.cloned.1.call-update) | async-done | bytes 2560016 | tf_op jit(solution)/shard_map/reduce_scatter | solution.py:286
  1420.8 162.0 %reduce-scatter.36.cloned.1.call-done = bf16[1600,600]{0,1:T(8,128)(2,1)} async-done(((bf16[1600,4800]{0,1:T(8,128)(2,1)}), bf16[1600,600]{0,1:T(8,128)(2,1)}) %reduce-scatter.36.cloned.1.call-update) | async-done | bytes 1920016
  1585.4 32.6 %reduce-scatter.32.cloned.1.call-done = bf16[800,1]{1,0:T(8,128)(2,1)} async-done(((bf16[6400,1]{1,0:T(8,128)(2,1)}), bf16[800,1]{1,0:T(8,128)(2,1)}) %reduce-scatter.32.cloned.1.call-update) | async-done | bytes 1616
  1619.1 26.8 %reduce-scatter.30.cloned.1.call-done = bf16[400,200]{1,0:T(8,128)(2,1)} async-done(((bf16[1600,200]{1,0:T(8,128)(2,1)}), bf16[400,200]{1,0:T(8,128)(2,1)}) %reduce-scatter.30.cloned.1.call-update) | async-done | bytes 160016
  1648.1 12.9 fusion.47
  1661.1 28.6 %all-reduce.15 = (bf16[8,1600]{1,0:T(8,128)(2,1)S(1)}, bf16[1600]{0:T(1024)(128)(2,1)S(1)}) all-reduce(bf16[8,1600]{1,0:T(8,128)(2,1)S(1)} %stack.44, bf16[1600]{0:T(1024)(128)(2,1)S(1)} %dynamic-update-slice.8), channel_id=12, replica_groups=mesh['fsdp'=4,'ctx'=8] {'ctx'}, use_global_device_ids=true, to_apply=%region_26.27.clone | all-reduce | flops 14400 | bytes 57600
  1689.7 9.3 all-reduce.17
  1702.6 12.3 fusion.32
  1717.5 93.0 %all-reduce.21.cloned.1.call-done = (bf16[1600,600]{0,1:T(8,128)(2,1)}, bf16[1600,800]{0,1:T(8,128)(2,1)}) async-done(((bf16[1600,600]{0,1:T(8,128)(2,1)}, bf16[1600,800]{0,1:T(8,128)(2,1)}), (bf16[1600,600]{0,1:T(8,128)(2,1)}, bf16[1600,800]{0,1:T(8,128)(2,1)})) %all-reduce.21.cloned.1.call-update) | async-done | bytes 4480016
  (343 shorter events, 141.9 us)
Async XLA Ops:
  7.2 40.3 %all-gather.19.cloned.1.call-start = ((), (), s32[]{:S(2)}) async-start(), calls=%async_computation.8 | async-start | bytes 2560000 | tf_op jit(solution)/shard_map/all_gather | solution.py:95
  7.9 45.0 %copy-start.9 = (u32[32]{0:T(128)S(1)}, u32[32]{0:T(128)}, u32[]{:S(2)}) copy-start(u32[32]{0:T(128)} %constant.313) | copy-start | bytes 388
  7.9 46.9 %copy-start.11 = (bf16[200]{0:T(256)(128)(2,1)S(1)}, bf16[200]{0:T(256)(128)(2,1)}, u32[]{:S(2)}) copy-start(bf16[200]{0:T(256)(128)(2,1)} %param.30) | copy-start | bytes 1204
  7.9 47.2 %copy-start.12 = (bf16[200]{0:T(256)(128)(2,1)S(1)}, bf16[200]{0:T(256)(128)(2,1)}, u32[]{:S(2)}) copy-start(bf16[200]{0:T(256)(128)(2,1)} %param.31) | copy-start | bytes 1204
  7.9 47.4 %copy-start.13 = (bf16[200]{0:T(256)(128)(2,1)S(1)}, bf16[200]{0:T(256)(128)(2,1)}, u32[]{:S(2)}) copy-start(bf16[200]{0:T(256)(128)(2,1)} %param.29) | copy-start | bytes 1204
  8.0 47.7 %copy-start.14 = (bf16[200]{0:T(256)(128)(2,1)S(1)}, bf16[200]{0:T(256)(128)(2,1)}, u32[]{:S(2)}) copy-start(bf16[200]{0:T(256)(128)(2,1)} %param.23) | copy-start | bytes 1204
  8.0 47.9 %copy-start.15 = (bf16[200]{0:T(256)(128)(2,1)S(1)}, bf16[200]{0:T(256)(128)(2,1)}, u32[]{:S(2)}) copy-start(bf16[200]{0:T(256)(128)(2,1)} %param.24) | copy-start | bytes 1204
  8.0 48.2 %copy-start.16 = (bf16[200]{0:T(256)(128)(2,1)S(1)}, bf16[200]{0:T(256)(128)(2,1)}, u32[]{:S(2)}) copy-start(bf16[200]{0:T(256)(128)(2,1)} %param.27) | copy-start | bytes 1204
  8.0 48.4 %copy-start.17 = (bf16[200]{0:T(256)(128)(2,1)S(1)}, bf16[200]{0:T(256)(128)(2,1)}, u32[]{:S(2)}) copy-start(bf16[200]{0:T(256)(128)(2,1)} %param.26) | copy-start | bytes 1204
  8.0 48.6 %copy-start.10 = (bf16[800]{0:T(1024)(128)(2,1)S(1)}, bf16[800]{0:T(1024)(128)(2,1)}, u32[]{:S(2)}) copy-start(bf16[800]{0:T(1024)(128)(2,1)} %param.33) | copy-start | bytes 4804
  8.0 79.3 %copy-start.2 = (bf16[1,128,1600]{1,2,0:T(8,128)(2,1)S(1)}, bf16[1,128,1600]{1,2,0:T(8,128)(2,1)}, u32[]{:S(2)}) copy-start(bf16[1,128,1600]{1,2,0:T(8,128)(2,1)} %param.20) | copy-start | bytes 1228804
  8.0 189.2 %all-gather.21.cloned.1.call-start = ((), (), s32[]{:S(2)}) async-start(), calls=%async_computation.9 | async-start | bytes 17971200 | tf_op jit(solution)/shard_map/all_gather | solution.py:101
  51.6 190.1 %all-gather.27.cloned.1.call-start = ((), (), s32[]{:S(2)}) async-start(), calls=%async_computation.12 | async-start | bytes 3584000 | tf_op jit(solution)/shard_map/all_gather | solution.py:97
  52.3 231.0 %all-gather.33.cloned.1.call-start = ((), (), s32[]{:S(2)}) async-start(), calls=%async_computation.16 | async-start | bytes 3328000 | tf_op jit(solution)/shard_map/all_gather | solution.py:98
  52.9 299.8 %all-gather.23.cloned.1.call-start = ((), (), s32[]{:S(2)}) async-start(), calls=%async_computation.10 | async-start | bytes 7372800 | tf_op jit(solution)/shard_map/all_gather | solution.py:167
  87.8 121.5 %copy-start.8 = (bf16[400,200]{1,0:T(8,128)(2,1)S(1)}, bf16[400,200]{1,0:T(8,128)(2,1)}, u32[]{:S(2)}) copy-start(bf16[400,200]{1,0:T(8,128)(2,1)} %param.28) | copy-start | bytes 480004
  209.3 200.5 %all-gather.25.cloned.1.call-start = ((), (), s32[]{:S(2)}) async-start(), calls=%async_computation.11 | async-start | bytes 5990400 | tf_op jit(solution)/shard_map/all_gather | solution.py:102
  225.6 372.7 %all-gather.29.cloned.1.call-start = ((), (), s32[]{:S(2)}) async-start(), calls=%async_computation.13 | async-start | bytes 23961600 | tf_op jit(solution)/shard_map/all_gather | solution.py:103
  246.8 532.9 %all-gather.31.cloned.1.call-start = ((), (), s32[]{:S(2)}) async-start(), calls=%async_computation.14 | async-start | bytes 23040000 | tf_op jit(solution)/shard_map/all_gather | solution.py:104
  289.6 652.2 %reduce-scatter.28.cloned.1.call-start = ((), (), s32[]{:S(2)}) async-start(), calls=%async_computation.17 | async-start | bytes 7372800
  414.2 365.5 %copy-start.4 = (bf16[1,128,1600]{1,2,0:T(8,128)(2,1)S(1)}, bf16[1,128,1600]{1,2,0:T(8,128)(2,1)}, u32[]{:S(2)}) copy-start(bf16[1,128,1600]{1,2,0:T(8,128)(2,1)} %param.22) | copy-start | bytes 1228804
  871.2 132.4 %reduce-scatter.38.cloned.1.call-start = ((), (), s32[]{:S(2)}) async-start(), calls=%async_computation.22 | async-start | bytes 5990400
  876.4 332.4 %reduce-scatter.40.cloned.1.call-start = ((), (), s32[]{:S(2)}) async-start(), calls=%async_computation.23 | async-start | bytes 23040000
  889.2 531.6 %reduce-scatter.26.cloned.1.call-start = ((), (), s32[]{:S(2)}) async-start(), calls=%async_computation.15 | async-start | bytes 23961600 | tf_op jit(solution)/shard_map/reduce_scatter | solution.py:286
  900.7 42.8 %copy-start.3 = (bf16[1,128,1600]{1,2,0:T(8,128)(2,1)S(1)}, bf16[1,128,1600]{1,2,0:T(8,128)(2,1)}, u32[]{:S(2)}) copy-start(bf16[1,128,1600]{1,2,0:T(8,128)(2,1)} %param.20) | copy-start | bytes 1228804
  900.7 682.1 %reduce-scatter.36.cloned.1.call-start = ((), (), s32[]{:S(2)}) async-start(), calls=%async_computation.21 | async-start | bytes 17971200
  954.6 663.4 %reduce-scatter.32.cloned.1.call-start = ((), (), s32[]{:S(2)}) async-start(), calls=%async_computation.19 | async-start | bytes 1843200
  958.7 687.2 %reduce-scatter.30.cloned.1.call-start = ((), (), s32[]{:S(2)}) async-start(), calls=%async_computation.18 | async-start | bytes 1024000
  1005.8 709.0 %reduce-scatter.34.cloned.1.call-start = ((), (), s32[]{:S(2)}) async-start(), calls=%async_computation.20 | async-start | bytes 4096000
  1213.5 369.3 %copy-start.20 = (u32[32]{0:T(128)S(1)}, u32[32]{0:T(128)}, u32[]{:S(2)}) copy-start(u32[32]{0:T(128)} %constant.376) | copy-start | bytes 388
  1213.6 371.4 %copy-start.19 = (bf16[200]{0:T(256)(128)(2,1)S(1)}, bf16[200]{0:T(256)(128)(2,1)}, u32[]{:S(2)}) copy-start(bf16[200]{0:T(256)(128)(2,1)} %param.35) | copy-start | bytes 1204
  1213.6 596.9 %all-reduce.21.cloned.1.call-start = ((), (), s32[]{:S(2)}) async-start(), calls=%async_computation.24 | async-start | bytes 9318400
  (6 other events, 13.1 us)
Sparse Core Ops, SparseCore 0:
  9.9 37.5 all-gather.18
  51.7 145.4 all-gather.20
  199.1 42.5 all-gather.26
  243.3 39.9 all-gather.32
  285.3 67.3 all-gather.22
  354.8 54.9 all-gather.24
  411.4 186.8 all-gather.28
  600.0 179.6 all-gather.30
  871.3 70.4 reduce-scatter.27
  943.9 59.5 reduce-scatter.37
  1005.9 202.9 reduce-scatter.39
  1211.1 209.6 reduce-scatter.25
  1423.2 159.6 reduce-scatter.35
  1585.1 32.8 reduce-scatter.31
  1621.6 24.2 reduce-scatter.29
  1649.0 45.1 reduce-scatter.33
  1698.0 112.4 all-reduce.20
where the time goes:
time: 1830 us; the launch traced here: 1820 us
  waiting for transfers between devices  1460 us (80%)
  matrix products  155 us (8%)
  blocking collectives  83.4 us (5%)
  local copies, waits for them, and re-layouts  78.3 us (4%)
  other arithmetic  26.4 us (1%)
    unnamed x25, waiting for transfers between devices  604 us
    reduce_scatter x1, waiting for transfers between devices, body(): lax.psum_scatter(jnp.einsum('td,te->de', hidden_two, d_before, preferred_...  207 us
    all_gather x1, waiting for transfers between devices, body(): lax.all_gather(fc_rows, 'ctx', axis=1, tiled=True)  184 us
    all_gather x1, waiting for transfers between devices, body(): lax.all_gather(proj_rows, 'ctx', axis=1, tiled=True)  168 us
    all_gather x1, waiting for transfers between devices, body(): lax.all_gather(qkv_rows, 'ctx', axis=1, tiled=True)  109 us
    all_gather x1, waiting for transfers between devices, body(): shard_rows = lax.all_gather(key_value, 'ctx', axis=0, tiled=True)  61.8 us
    unnamed x2, blocking collectives  58.9 us
    all_gather x1, waiting for transfers between devices, body(): lax.all_gather(qkv_weight, 'fsdp', axis=0, tiled=True)  39.4 us
  transfers between devices with their start and end apart: 17, of which 16 were waited for; matrix products, arithmetic and copies ran while one was open for 9% of the time, Pallas kernels for 0%

commit v1 on v0

v1 whole, which is shorter than its diff:
```python
from functools import partial
import math

import jax
import jax.numpy as jnp
from jax import lax
from jax.experimental import pallas as pl
from jax.experimental.pallas import tpu as pltpu
from jax.sharding import Mesh
from jax.sharding import PartitionSpec as P

HD = 64
EPS = 1e-05
FLOOR = -1e30
BF = jnp.bfloat16
F32 = jnp.float32
CTX = ("z", "core")


def dot(a, b):
    return jnp.dot(a, b, preferred_element_type=F32)


def dot_nt(a, b):
    return lax.dot_general(a, b, (((1,), (1,)), ((), ())), preferred_element_type=F32)


def dot_tn(a, b):
    return lax.dot_general(a, b, (((0,), (0,)), ((), ())), preferred_element_type=F32)


def norm_rows(rows):
    centred = rows - jnp.mean(rows, axis=-1, keepdims=True)
    rstd = lax.rsqrt(jnp.mean(centred * centred, axis=-1, keepdims=True) + EPS)
    return centred * rstd, rstd


def norm_back(upstream, xhat, rstd, gain):
    inner = upstream * gain
    return rstd * (
        inner
        - jnp.mean(inner, axis=-1, keepdims=True)
        - xhat * jnp.mean(inner * xhat, axis=-1, keepdims=True)
    )


def positions(order_table, rows, block_rows):
    stored = jnp.arange(rows, dtype=jnp.int32)
    picked = jnp.repeat(order_table, block_rows, total_repeat_length=rows)
    return picked * block_rows + stored % block_rows


def attend_kernel(heads, q_block, qkv_ref, pos_col_ref, pos_row_ref, out_ref, lse_ref):
    rows = qkv_ref.shape[0]
    width = heads * HD
    for h in range(heads):
        k = qkv_ref[:, width + h * HD : width + (h + 1) * HD]
        v = qkv_ref[:, 2 * width + h * HD : 2 * width + (h + 1) * HD]
        for b in range(rows // q_block):
            at = slice(b * q_block, (b + 1) * q_block)
            q = qkv_ref[at, h * HD : (h + 1) * HD] * BF(HD**-0.5)
            s = dot_nt(k, q)
            s = jnp.where(pos_col_ref[...] <= pos_row_ref[:, at], s, FLOOR)
            top = jnp.max(s, axis=0, keepdims=True)
            p = jnp.exp(s - top)
            total = jnp.sum(p, axis=0, keepdims=True)
            o = dot_tn(v, p.astype(BF)) * (1.0 / total)
            out_ref[at, h * HD : (h + 1) * HD] = o.T.astype(BF)
            lse_ref[h : h + 1, at] = top + jnp.log(total)


def attend(qkv, pos, heads):
    rows = qkv.shape[0]
    return pl.pallas_call(
        partial(attend_kernel, heads, min(256, rows)),
        out_shape=(
            jax.ShapeDtypeStruct((rows, heads * HD), BF),
            jax.ShapeDtypeStruct((heads, rows), F32),
        ),
        name="attend",
        compiler_params=pltpu.CompilerParams(vmem_limit_bytes=48 * 2**20),
    )(qkv, pos[:, None], pos[None, :])


def attend_back_kernel(
    heads, q_block, qkv_ref, pos_col_ref, pos_row_ref, out_ref, lse_ref, dout_ref, dqkv_ref, acc_ref
):
    rows = qkv_ref.shape[0]
    width = heads * HD
    for h in range(heads):
        k = qkv_ref[:, width + h * HD : width + (h + 1) * HD]
        v = qkv_ref[:, 2 * width + h * HD : 2 * width + (h + 1) * HD]
        for b in range(rows // q_block):
            at = slice(b * q_block, (b + 1) * q_block)
            q = qkv_ref[at, h * HD : (h + 1) * HD] * BF(HD**-0.5)
            do = dout_ref[at, h * HD : (h + 1) * HD]
            o = out_ref[at, h * HD : (h + 1) * HD]
            delta = jnp.sum(do.astype(F32).T * o.astype(F32).T, axis=0, keepdims=True)
            s = dot_nt(k, q)
            p = jnp.where(
                pos_col_ref[...] <= pos_row_ref[:, at], jnp.exp(s - lse_ref[h : h + 1, at]), 0.0
            )
            dp = dot_nt(v, do)
            ds = (p * (dp - delta)).astype(BF)
            dq = dot_tn(k, ds) * (HD**-0.5)
            dqkv_ref[at, h * HD : (h + 1) * HD] = dq.T.astype(BF)
            dk = dot(ds, q)
            dv = dot(p.astype(BF), do)
            if b == 0:
                acc_ref[:, :HD] = dk
                acc_ref[:, HD:] = dv
            else:
                acc_ref[:, :HD] += dk
                acc_ref[:, HD:] += dv
        dqkv_ref[:, width + h * HD : width + (h + 1) * HD] = acc_ref[:, :HD].astype(BF)
        dqkv_ref[:, 2 * width + h * HD : 2 * width + (h + 1) * HD] = acc_ref[:, HD:].astype(BF)


def attend_back(qkv, pos, out, lse, dout, heads):
    rows = qkv.shape[0]
    return pl.pallas_call(
        partial(attend_back_kernel, heads, min(256, rows)),
        out_shape=jax.ShapeDtypeStruct((rows, 3 * heads * HD), BF),
        scratch_shapes=[pltpu.VMEM((rows, 2 * HD), F32)],
        name="attend_back",
        compiler_params=pltpu.CompilerParams(vmem_limit_bytes=48 * 2**20),
    )(qkv, pos[:, None], pos[None, :], out, lse, dout)


MESH = pl.DeviceIdType.MESH


def remote(src, dst, send, recv, **to):
    return pltpu.make_async_remote_copy(
        src_ref=src, dst_ref=dst, send_sem=send, recv_sem=recv, device_id=to, device_id_type=MESH
    )


def lane_cuts(lanes, parts):
    tiles = -(-lanes // 128)
    return [min(lanes, (i * tiles + parts // 2) // parts * 128) for i in range(parts + 1)]


def column_segments(ranks, d, width, grain):
    own = 3 * d // ranks
    runs = []
    for src in range(ranks):
        for part in range(3):
            for dst in range(ranks):
                low = part * d + dst * width
                first = max(src * own, low)
                last = min((src + 1) * own, low + width, (part + 1) * d)
                if first < last:
                    at = part * width + first - low
                    runs.append(
                        (src, (first - src * own) // grain, dst, at // grain, (last - first) // grain)
                    )
    return runs


def meet(peers):
    barrier = pltpu.get_barrier_semaphore()
    for peer in peers:
        pl.semaphore_signal(barrier, inc=1, device_id=peer, device_id_type=MESH)
    pl.semaphore_wait(barrier, len(peers))


class Line:
    def __init__(self, buf, size, sems):
        self.buf, self.size = buf, size
        self.right, self.left, self.recv = sems
        self.z = lax.axis_index("z")

    def copy(self, block, way):
        send = (self.right if way > 0 else self.left).at[block]
        at = self.buf(block)
        return remote(at, at, send, self.recv.at[block], z=self.z + way)

    def start(self):
        @pl.when(self.z < self.size - 1)
        def _():
            self.copy(self.z, 1).start()

        @pl.when(self.z > 0)
        def _():
            self.copy(self.z, -1).start()

    def step(self, s, then=None):
        @pl.when(self.z >= s)
        def _():
            block = self.z - s
            self.copy(block, 1).wait_recv()

            @pl.when(self.z < self.size - 1)
            def _():
                self.copy(block, 1).start()

            if then is not None:
                then(block)

        @pl.when(self.z + s < self.size)
        def _():
            block = self.z + s
            self.copy(block, -1).wait_recv()

            @pl.when(self.z > 0)
            def _():
                self.copy(block, -1).start()

            if then is not None:
                then(block)

    def finish(self):
        for s in range(self.size):

            @pl.when((self.z >= s) & (self.z < self.size - 1))
            def _():
                self.copy(self.z - s, 1).wait_send()

            @pl.when((self.z + s < self.size) & (self.z > 0))
            def _():
                self.copy(self.z + s, -1).wait_send()


def start_kernel(
    cfg,
    tok,
    wq,
    small,
    pj,
    pos_col,
    pos_row,
    h1,
    w,
    qkv,
    att,
    lse,
    smalls,
    p2,
    toks,
    p1,
    vecs,
    small_send,
    small_recv,
    q_send,
    q_recv,
    q_local,
    x_send,
    x_recv,
    t_right,
    t_left,
    t_recv,
    c_send,
    c_recv,
    p1_send,
    p1_recv,
    p2_send,
    p2_recv,
    p_local,
):
    fs, nz, d, heads = cfg
    cs = 2 * nz
    f, z, core = lax.axis_index("fsdp"), lax.axis_index("z"), lax.axis_index("core")
    rank = 2 * z + core
    rows, lanes = tok.shape[0], wq.shape[2]
    width = heads * HD
    grain = wq.shape[1]
    own_rows = d // fs
    part = d // cs
    my_lanes = pl.ds(pl.multiple_of(f * lanes, 128), lanes)
    runs = column_segments(cs, d, width, grain)
    cuts = lane_cuts(pj.shape[1], fs)

    w[:, :, my_lanes] = jnp.zeros((w.shape[0], grain, lanes), BF)
    ranks = [lax.rem(rank + i, cs) for i in range(1, cs)]
    planes = [lax.rem(f + i, fs) for i in range(1, fs)]
    meet([dict(z=r // 2, core=lax.rem(r, 2)) for r in ranks] + [dict(fsdp=p) for p in planes])

    def run_copy(n):
        src, first, dst, at, count = runs[n]
        here, there = wq.at[pl.ds(first, count)], w.at[pl.ds(at, count), :, my_lanes]
        return remote(here, there, q_send.at[n], q_recv.at[n], z=dst // 2, core=dst % 2)

    for n, (src, first, dst, at, count) in enumerate(runs):

        @pl.when(rank == src)
        def _():
            if src == dst:
                here, there = wq.at[pl.ds(first, count)], w.at[pl.ds(at, count), :, my_lanes]
                pltpu.make_async_copy(here, there, q_local.at[n]).start()
            else:
                run_copy(n).start()

    def small_copy(i):
        r = ranks[i]
        at = smalls.at[rank]
        return remote(small, at, small_send.at[i], small_recv.at[rank], z=r // 2, core=lax.rem(r, 2))

    for i in range(cs - 1):
        small_copy(i).start()

    def p1_copy(g):
        at = pl.ds(cuts[g], cuts[g + 1] - cuts[g])
        to = p1.at[f, :, pl.ds(0, cuts[g + 1] - cuts[g])]
        return remote(pj.at[:, at], to, p1_send.at[g], p1_recv.at[f], fsdp=g)

    def p1_arrival(g, src):
        to = p1.at[src, :, pl.ds(0, cuts[g + 1] - cuts[g])]
        return remote(to, to, p1_send.at[g], p1_recv.at[src], fsdp=src)

    def p1_local(g):
        at = pl.ds(cuts[g], cuts[g + 1] - cuts[g])
        to = p1.at[f, :, pl.ds(0, cuts[g + 1] - cuts[g])]
        return pltpu.make_async_copy(pj.at[:, at], to, p_local.at[0])

    for g in range(fs):
        if cuts[g] == cuts[g + 1]:
            continue

        @pl.when(f == g)
        def _():
            p1_local(g).start()

        @pl.when(f != g)
        def _():
            p1_copy(g).start()

    for n, (src, first, dst, at, count) in enumerate(runs):

        @pl.when(rank == dst)
        def _():
            if src == dst:
                here, there = wq.at[pl.ds(first, count)], w.at[pl.ds(at, count), :, my_lanes]
                pltpu.make_async_copy(here, there, q_local.at[n]).wait()
            else:
                run_copy(n).wait_recv()

    def x_copy(i, peer):
        at = w.at[:, :, my_lanes]
        return remote(at, at, x_send.at[i], x_recv.at[f], fsdp=peer)

    def x_arrival(peer):
        at = w.at[:, :, pl.ds(pl.multiple_of(peer * lanes, 128), lanes)]
        return remote(at, at, x_send.at[0], x_recv.at[peer], fsdp=peer)

    for i, peer in enumerate(planes):
        x_copy(i, peer).start()

    pltpu.sync_copy(tok, toks.at[rank])
    line = Line(lambda b: toks.at[2 * b + core], nz, (t_right, t_left, t_recv))

    def pass_on(block):
        at = toks.at[2 * block + core]
        return remote(at, at, c_send.at[block], c_recv.at[block], core=1 - core)

    def arrival(block):
        at = toks.at[2 * block + 1 - core]
        return remote(at, at, c_send.at[block], c_recv.at[block], core=1 - core)

    line.start()
    pass_on(z).start()

    smalls[rank] = small[...]
    vecs[...] = jnp.zeros(vecs.shape, F32)
    for i, r in enumerate(ranks):
        back = lax.rem(rank + cs - 1 - i, cs)
        remote(small, smalls.at[back], small_send.at[i], small_recv.at[back], z=z).wait_recv()
    for r in range(cs):
        vecs[:, part * r : part * (r + 1)] = smalls[r, 0:8, 0:part]
    for g in range(fs):
        h1[:, lanes * g + own_rows : lanes * (g + 1)] = jnp.zeros(
            (h1.shape[0], lanes - own_rows), BF
        )

    for s in range(1, nz):
        line.step(s, lambda b: pass_on(b).start())

    def p1_wait(src):
        for g in range(fs):
            if cuts[g] < cuts[g + 1]:

                @pl.when(f == g)
                def _():
                    p1_arrival(g, src).wait_recv()

    def p2_copy(plane):
        return remote(
            p1.at[plane], p2.at[z], p2_send.at[plane], p2_recv.at[z], z=plane
        )

    for g in range(fs):
        if cuts[g] < cuts[g + 1]:

            @pl.when(f == g)
            def _():
                p1_local(g).wait()

    for i in range(1, fs):
        p1_wait(lax.rem(f + fs - i, fs))
    for plane in range(nz):

        @pl.when(z == plane)
        def _():
            pltpu.make_async_copy(p1.at[plane], p2.at[z], p_local.at[1]).start()

        @pl.when(z != plane)
        def _():
            p2_copy(plane).start()

    for b in range(nz):
        arrival(b).wait_recv()

    step = 32

    def norm_chunk(i, _):
        block, at = i // (rows // step), lax.rem(i, rows // step) * step
        x = toks[block, pl.ds(at, step), :].astype(F32)
        xhat, _ = norm_rows(x)
        h = (xhat * vecs[0:1, 0:d] + vecs[1:2, 0:d]).astype(BF)
        to = pl.ds(pl.multiple_of(i * step, step), step)
        for g in range(fs):
            h1[to, lanes * g : lanes * g + own_rows] = h[:, own_rows * g : own_rows * (g + 1)]
        return 0

    lax.fori_loop(0, cs * rows // step, norm_chunk, 0)

    for i in range(1, fs):
        x_arrival(lax.rem(f + fs - i, fs)).wait_recv()

    tall = min(256, cs * rows)
    head_lanes = pl.ds(pl.multiple_of(rank * width, 128), width)

    def project(i, _):
        at = pl.ds(pl.multiple_of(i * tall, tall), tall)
        full = dot_nt(h1[at, :], w[...].reshape(3 * width, fs * lanes))
        qkv[at, 0:width] = (full[:, 0:width] + vecs[2:3, head_lanes]).astype(BF)
        qkv[at, width : 2 * width] = full[:, width : 2 * width].astype(BF)
        qkv[at, 2 * width :] = (full[:, 2 * width :] + vecs[3:4, head_lanes]).astype(BF)
        return 0

    lax.fori_loop(0, cs * rows // tall, project, 0)
    attend_kernel(heads, tall, qkv, pos_col, pos_row, att, lse)

    for n, (src, first, dst, at, count) in enumerate(runs):
        if src != dst:

            @pl.when(rank == src)
            def _():
                run_copy(n).wait_send()

    for i in range(cs - 1):
        small_copy(i).wait_send()
    for i, peer in enumerate(planes):
        x_copy(i, peer).wait_send()
    line.finish()
    for b in range(nz):
        pass_on(b).wait_send()
    for g in range(fs):
        if cuts[g] < cuts[g + 1]:

            @pl.when(f != g)
            def _():
                p1_copy(g).wait_send()

    for plane in range(nz):

        @pl.when(z == plane)
        def _():
            pltpu.make_async_copy(p1.at[plane], p2.at[z], p_local.at[1]).wait()

        @pl.when(z != plane)
        def _():
            p2_copy(plane).wait_send()
            remote(p1.at[plane], p2.at[plane], p2_send.at[plane], p2_recv.at[plane], z=plane).wait_recv()


def start(cfg, tok, wq, small, pj, pos):
    fs, nz, d, heads = cfg
    cs = 2 * nz
    rows, lanes = tok.shape[0], wq.shape[2]
    width, length = heads * HD, rows * cs
    cuts = lane_cuts(pj.shape[1], fs)
    slab = max(b - a for a, b in zip(cuts, cuts[1:]))
    runs = len(column_segments(cs, d, width, wq.shape[1]))
    vmem = pl.BlockSpec(memory_space=pltpu.VMEM)
    hbm = pl.BlockSpec(memory_space=pl.ANY)
    sem = lambda n: pltpu.SemaphoreType.DMA((n,))
    return pl.pallas_call(
        partial(start_kernel, cfg),
        out_shape=(
            jax.ShapeDtypeStruct((length, fs * lanes), BF),
            jax.ShapeDtypeStruct((3 * width // wq.shape[1], wq.shape[1], fs * lanes), BF),
            jax.ShapeDtypeStruct((length, 3 * width), BF),
            jax.ShapeDtypeStruct((length, width), BF),
            jax.ShapeDtypeStruct((heads, length), F32),
            jax.ShapeDtypeStruct((cs,) + small.shape, F32),
            jax.ShapeDtypeStruct((nz, pj.shape[0], slab), BF),
        ),
        in_specs=[vmem, vmem, vmem, hbm, vmem, vmem],
        out_specs=(vmem, vmem, vmem, vmem, vmem, vmem, hbm),
        scratch_shapes=[
            pltpu.VMEM((cs, rows, d), BF),
            pltpu.VMEM((fs, pj.shape[0], slab), BF),
            pltpu.VMEM((8, width * cs), F32),
            sem(cs),
            sem(cs),
            sem(runs),
            sem(runs),
            sem(runs),
            sem(fs),
            sem(fs),
            sem(nz),
            sem(nz),
            sem(nz),
            sem(nz),
            sem(nz),
            sem(fs),
            sem(fs),
            sem(nz),
            sem(nz),
            sem(2),
        ],
        name="start",
        compiler_params=pltpu.CompilerParams(
            collective_id=0, has_side_effects=True, vmem_limit_bytes=56 * 2**20
        ),
    )(tok, wq, small, pj, pos[:, None], pos[None, :])


def body(
    tokens,
    block_order,
    cotangent,
    pre_attn_gain,
    pre_attn_bias,
    qkv_weight,
    query_bias,
    value_bias,
    out_weight,
    out_bias,
    pre_mlp_gain,
    pre_mlp_bias,
    fc_weight,
    fc_bias,
    proj_weight,
    proj_bias,
):
    fs, nz = lax.axis_size("fsdp"), lax.axis_size("z")
    cs = nz * 2
    rank = lax.axis_index("z") * 2 + lax.axis_index("core")
    rows, d = tokens.shape[1], tokens.shape[2]
    length = rows * cs
    heads_all = d // HD
    heads = -(-heads_all // cs)
    width = heads * HD
    padded = width * cs
    ff_chip = fc_weight.shape[1] * 2

    part, own_rows = d // cs, d // fs
    up = lambda n: -(-n // 128) * 128
    small = jnp.concatenate(
        [
            pre_attn_gain,
            pre_attn_bias,
            query_bias,
            value_bias,
            out_bias,
            pre_mlp_gain,
            pre_mlp_bias,
            proj_bias,
            fc_bias,
        ]
    ).astype(F32)
    small = jnp.pad(small.reshape(-1, part), ((0, 0), (0, up(part) - part)))
    lanes = up(own_rows)
    wq = jnp.pad(qkv_weight.T, ((0, 0), (0, lanes - own_rows)))
    grain = math.gcd(math.gcd(wq.shape[0], HD), 8)
    wq = wq.reshape(-1, grain, lanes)
    pj = jnp.pad(proj_weight.T, ((0, 0), (0, up(ff_chip) - ff_chip)))
    pos = positions(block_order, length, length // block_order.shape[0])
    h1, w, qkv, att, lse, smalls, p2 = start((fs, nz, d, heads), tokens[0], wq, small, pj, pos)
    vec = lambda i: smalls[:, i, :part].reshape(d)
    gain1, ob, gain2, shift2, pb = vec(0), vec(4), vec(5), vec(6), vec(7)
    fb = smalls[:, 8:, :part].reshape(cs, -1)
    fb_chip = lax.dynamic_slice_in_dim(fb, lax.axis_index("z") * 2, 2, 0).reshape(ff_chip)
    w = w.reshape(3 * width, fs * lanes)

    w_out = lax.all_gather(
        lax.all_gather(out_weight, CTX, axis=1, tiled=True), "fsdp", axis=0, tiled=True
    )
    fc = lax.all_gather(fc_weight, "fsdp", axis=0, tiled=True)
    fc = lax.all_gather(fc, "core", axis=1, tiled=True)
    cuts = lane_cuts(pj.shape[1], fs)
    pj_all = lax.all_gather(p2, "fsdp", axis=0)
    pj_all = jnp.concatenate([pj_all[g, :, :, : cuts[g + 1] - cuts[g]] for g in range(fs)], axis=2)
    pj_all = lax.all_gather(pj_all, "core", axis=1).reshape(d, -1)[:, :ff_chip]

    own = tokens[0].astype(F32)
    att_own = lax.all_to_all(att, CTX, split_axis=0, concat_axis=1, tiled=True)[:, :d]
    middle = own + dot(att_own, w_out) + ob

    xhat2, rstd2 = norm_rows(middle)
    h2_own = (xhat2 * gain2 + shift2).astype(BF)
    h2 = lax.all_gather(h2_own, "z", axis=0, tiled=True)
    ct = lax.all_gather(cotangent[0], "z", axis=0, tiled=True)
    before = dot(h2, fc) + fb_chip
    act, gelu_back = jax.vjp(partial(jax.nn.gelu, approximate=True), before)
    act = act.astype(BF)
    d_before = gelu_back(dot(ct, pj_all))[0].astype(BF)
    out_part = dot_nt(act, pj_all).astype(BF)
    dh2_part = dot_nt(d_before, fc).astype(BF)
    out_rows = lax.psum_scatter(out_part, "z", scatter_dimension=0, tiled=True)
    output = (middle + out_rows.astype(F32) + pb).astype(BF)
    dh2 = lax.psum_scatter(dh2_part, "z", scatter_dimension=0, tiled=True).astype(F32)

    fc_grad = lax.psum_scatter(
        dot_tn(h2, d_before).astype(BF), "core", scatter_dimension=1, tiled=True
    )
    fc_grad = lax.psum_scatter(fc_grad, "fsdp", scatter_dimension=0, tiled=True)
    proj_grad = dot_tn(act, ct).astype(BF)
    full = jnp.zeros((ff_chip * nz, d), BF)
    full = lax.dynamic_update_slice_in_dim(full, proj_grad, lax.axis_index("z") * ff_chip, 0)
    proj_grad = lax.psum_scatter(full, "fsdp", scatter_dimension=0, tiled=True)
    proj_grad = lax.psum_scatter(proj_grad, CTX, scatter_dimension=1, tiled=True)

    ct_own = cotangent[0].astype(F32)
    d_middle = ct_own + norm_back(dh2, xhat2, rstd2, gain2)
    d_branch = d_middle.astype(BF)
    out_grad = dot_tn(att_own, d_branch).astype(BF)
    out_grad = lax.psum_scatter(out_grad, CTX, scatter_dimension=1, tiled=True)
    out_grad = lax.psum_scatter(out_grad, "fsdp", scatter_dimension=0, tiled=True)
    d_att_own = dot_nt(d_branch, w_out).astype(BF)
    d_att_own = jnp.pad(d_att_own, ((0, 0), (0, padded - d)))
    d_att = lax.all_to_all(d_att_own, CTX, split_axis=1, concat_axis=0, tiled=True)
    d_qkv = attend_back(qkv, pos, att, lse, d_att, heads)
    dh1_part = dot(d_qkv, w).astype(BF).reshape(length, fs, lanes)
    dh1_part = dh1_part[:, :, :own_rows].reshape(length, d)
    dh1 = lax.psum_scatter(dh1_part, CTX, scatter_dimension=0, tiled=True).astype(F32)
    xhat1, rstd1 = norm_rows(own)
    input_grad = d_middle + norm_back(dh1, xhat1, rstd1, gain1)

    qkv_grad = dot_tn(h1, d_qkv).astype(BF).reshape(fs, lanes, 3 * width)
    qkv_grad = qkv_grad[:, :own_rows].reshape(d, 3 * width)
    qkv_grad = lax.psum_scatter(qkv_grad, "fsdp", scatter_dimension=0, tiled=True)
    full = jnp.zeros((qkv_grad.shape[0], 3, padded), BF)
    full = lax.dynamic_update_slice_in_dim(
        full, qkv_grad.reshape(-1, 3, width), rank * width, 2
    )
    qkv_grad = lax.psum_scatter(
        full[:, :, :d].reshape(-1, 3 * d), CTX, scatter_dimension=1, tiled=True
    )

    bias_cols = jnp.sum(d_qkv.astype(F32), axis=0).reshape(3, width)
    bias_full = jnp.zeros((3, padded), F32)
    bias_full = lax.dynamic_update_slice_in_dim(bias_full, bias_cols, rank * width, 1)[:, :d]
    fb_full = jnp.zeros((nz, ff_chip), F32)
    fb_full = lax.dynamic_update_slice_in_dim(
        fb_full, jnp.sum(d_before.astype(F32), axis=0)[None], lax.axis_index("z"), 0
    )
    stack = jnp.stack(
        [
            jnp.sum(dh1 * xhat1, axis=0),
            jnp.sum(dh1, axis=0),
            bias_full[0],
            bias_full[2],
            jnp.sum(d_branch.astype(F32), axis=0),
            jnp.sum(dh2 * xhat2, axis=0),
            jnp.sum(dh2, axis=0),
            jnp.sum(ct_own, axis=0),
        ]
    )
    stack = jnp.concatenate(
        [stack.reshape(8, cs, part).transpose(1, 0, 2).reshape(cs, -1), fb_full.reshape(cs, -1)],
        axis=1,
    )
    stack = lax.psum(lax.psum_scatter(stack, CTX, scatter_dimension=0, tiled=True), "fsdp")[0]
    g = [stack[i * part : (i + 1) * part] for i in range(8)]
    fb_grad = stack[8 * part :]
    return (
        output[None],
        input_grad[None],
        g[0],
        g[1],
        qkv_grad.astype(F32),
        g[2],
        g[3],
        out_grad.astype(F32),
        g[4],
        g[5],
        g[6],
        fc_grad.astype(F32),
        fb_grad,
        proj_grad.astype(F32),
        g[7],
    )


def solution(mesh):
    fs, cs = mesh.shape["fsdp"], mesh.shape["ctx"]
    split = Mesh(mesh.devices.reshape(fs, cs // 2, 2), ("fsdp", "z", "core"))
    rows = P("fsdp", CTX, None)
    weight = P("fsdp", CTX)
    vector = P(CTX)
    in_specs = (
        rows,
        P(),
        rows,
        vector,
        vector,
        weight,
        vector,
        vector,
        weight,
        vector,
        vector,
        vector,
        weight,
        vector,
        weight,
        vector,
    )
    out_specs = (
        rows,
        rows,
        vector,
        vector,
        weight,
        vector,
        vector,
        weight,
        vector,
        vector,
        vector,
        weight,
        vector,
        weight,
        vector,
    )
    return jax.shard_map(body, mesh=split, in_specs=in_specs, out_specs=out_specs, check_vma=False)
```

time: 1830 us -> 1160 us (0.63)
  waiting for transfers between devices: 1460 us -> 721 us
  Pallas kernels: 0 us -> 105 us
  local copies, waits for them, and re-layouts: 78.3 us -> 180 us
  matrix products: 155 us -> 65.6 us
  blocking collectives: 83.4 us -> 28.2 us
    all_gather x8, waiting for transfers between devices: 649 us -> 173 us  [the longest x1 42.4 us: body(): h2 = lax.all_gather(h2_own, 'z', axis=0, tiled=True)]
    unnamed x25 -> x27, waiting for transfers between devices: 604 us -> 430 us
    pallas_call x0 -> x2, Pallas kernels: none -> 105 us  [the longest x1 92 us: start(): pl.pallas_call(partial(start_kernel, cfg), out_shape=(jax.ShapeDtypeStruc...]
    reduce_scatter x1 -> x5, waiting for transfers between devices: 207 us -> 103 us  [the longest x1 38.1 us: body(): lax.psum_scatter(qkv_grad, 'fsdp', scatter_dimension=0, tiled=True)]
    dot_general x68 -> x11, matrix products: 155 us -> 65.6 us  [the longest x4 26 us: dot(): return jnp.dot(a, b, preferred_element_type=F32)]
    unnamed x2 -> x0, blocking collectives: 58.9 us -> none
    dynamic_update_slice x0 -> x4, local copies, waits for them, and re-layouts: none -> 48.2 us  [the longest x1 47.6 us: body(): lax.dynamic_update_slice_in_dim(full, proj_grad, lax.axis_index('z') * ff...]
    unnamed x74 -> x85, local copies, waits for them, and re-layouts: 38.2 us -> 72.4 us
  transfers between devices with their start and end apart: 17 -> 21, of which waited for: 16 -> 18; matrix products, arithmetic and copies ran while one was open for 9% -> 19% of each run, Pallas kernels for 0% -> 8%
where the time goes in v1:
time: 1160 us; the launch traced here: 1150 us
  waiting for transfers between devices  721 us (62%)
  local copies, waits for them, and re-layouts  180 us (16%)
  Pallas kernels  105 us (9%)
  matrix products  65.6 us (6%)
  other arithmetic  29 us (2%)
  blocking collectives  28.2 us (2%)
  between operations  15.9 us (1%)
    unnamed x27, waiting for transfers between devices  430 us
    pallas_call x1, Pallas kernels, start(): pl.pallas_call(partial(start_kernel, cfg), out_shape=(jax.ShapeDtypeStruc...  92 us
    unnamed x85, local copies, waits for them, and re-layouts  72.4 us
    dynamic_update_slice x1, local copies, waits for them, and re-layouts, body(): lax.dynamic_update_slice_in_dim(full, proj_grad, lax.axis_index('z') * ff...  47.6 us
    all_gather x1, waiting for transfers between devices, body(): h2 = lax.all_gather(h2_own, 'z', axis=0, tiled=True)  42.4 us
    all_gather x1, waiting for transfers between devices, body(): pj_all = lax.all_gather(p2, 'fsdp', axis=0)  41.1 us
    reduce_scatter x1, waiting for transfers between devices, body(): lax.psum_scatter(qkv_grad, 'fsdp', scatter_dimension=0, tiled=True)  38.1 us
    reduce_scatter x1, waiting for transfers between devices, body(): out_rows = lax.psum_scatter(out_part, 'z', scatter_dimension=0, tiled=True)  37.1 us
  transfers between devices with their start and end apart: 21, of which 18 were waited for; matrix products, arithmetic and copies ran while one was open for 19% of the time, Pallas kernels for 8%

profile of v1, /device:TPU:0, one launch (start us, length us, event | category | flops | bytes accessed | tf_op | source)
XLA Modules:
  0.0 1149.7 jit_solution(5553198274957783686)
XLA Ops:
  10.0 28.5 %all-gather.12.cloned.1.call-done = bf16[400,1600]{0,1:T(8,128)(2,1)} async-done(((bf16[400,200]{0,1:T(8,128)(2,1)}), bf16[400,1600]{0,1:T(8,128)(2,1)}) %all-gather.12.cloned.1.call-update) | async-done | bytes 1280016 | tf_op jit(solution)/shard_map/all_gather | solution.py:589
  50.8 5.8 select_select_fusion
  61.1 92.0 %start.1 = (bf16[1024,2048]{1,0:T(8,128)(2,1)}, bf16[96,8,2048]{2,1,0:T(8,128)(2,1)}, bf16[1024,768]{1,0:T(8,128)(2,1)}, bf16[1024,256]{1,0:T(8,128)(2,1)}, f32[...) custom-call(bf16[128,1600]{1,0:T(8,128)(2,1)} %bitcast.117, ...), custom_call_target="tpu_custom_call" | custom-call | tf_op jit(solution)/shard_map/start/pallas_call | solution.py:488
  163.6 14.8 %all-to-all-done = bf16[8,128,256]{1,2,0:T(8,128)(2,1)S(1)} async-done(((bf16[8,128,256]{1,2,0:T(8,128)(2,1)}), bf16[8,128,256]{1,2,0:T(8,128)(2,1)S(1)}, u32[]{:S(2)}, u32[]{:S(2)}) %all-to-all-start) | async-done | bytes 524320 | tf_op jit(solution)/shard_map/all_to_all | solution.py:599
  186.5 41.1 %all-gather.22.cloned.1.call-done = bf16[16,200,512]{2,1,0:T(8,128)(2,1)} async-done(((bf16[4,200,512]{2,1,0:T(8,128)(2,1)}), bf16[16,200,512]{2,1,0:T(8,128)(2,1)}) %all-gather.22.cloned.1.call-update) | async-done | bytes 3276816 | tf_op jit(solution)/shard_map/all_gather | solution.py:594
  232.4 12.0 %all-gather.20.cloned.1.call-done = bf16[1600,1600]{0,1:T(8,128)(2,1)} async-done(((bf16[1600,800]{0,1:T(8,128)(2,1)}), bf16[1600,1600]{0,1:T(8,128)(2,1)}) %all-gather.20.cloned.1.call-update) | async-done | bytes 5120016 | tf_op jit(solution)/shard_map/all_gather | solution.py:592
  244.4 42.4 %all-gather.16.cloned.1.call-done = bf16[512,1600]{1,0:T(8,128)(2,1)} async-done(((bf16[128,1600]{1,0:T(8,128)(2,1)}), bf16[512,1600]{1,0:T(8,128)(2,1)}) %all-gather.16.cloned.1.call-update) | async-done | bytes 1638416 | tf_op jit(solution)/shard_map/all_gather | solution.py:604
  286.8 7.9 convolution_add_fusion
  294.8 31.3 %all-gather.26.cloned.1.call-done = bf16[1,512,1600]{1,2,0:T(8,128)(2,1)} async-done(((bf16[1,128,1600]{1,2,0:T(8,128)(2,1)}), bf16[1,512,1600]{1,2,0:T(8,128)(2,1)}) %all-gather.26.cloned.1.call-update) | async-done | bytes 1638416 | tf_op jit(solution)/shard_map/all_gather | solution.py:605
  326.1 15.1 %all-gather.24.cloned.1.call-done = bf16[4,400,1664]{2,1,0:T(8,128)(2,1)} async-done(((bf16[4,200,1664]{2,1,0:T(8,128)(2,1)}), bf16[4,400,1664]{2,1,0:T(8,128)(2,1)}) %all-gather.24.cloned.1.call-update) | async-done | bytes 5324816 | tf_op jit(solution)/shard_map/all_gather | solution.py:596
  341.2 9.5 convert_reduce_fusion
  358.0 6.8 fusion.17
  368.8 27.5 %reduce-scatter.24.cloned.1.call-done = bf16[128,1600]{1,0:T(8,128)(2,1)} async-done(((bf16[512,1600]{1,0:T(8,128)(2,1)}), bf16[128,1600]{1,0:T(8,128)(2,1)}) %reduce-scatter.24.cloned.1.call-update) | async-done | bytes 409616 | tf_op jit(solution)/shard_map/reduce_scatter | solution.py:614
  397.6 37.1 %reduce-scatter.22.cloned.1.call-done = bf16[128,1600]{1,0:T(8,128)(2,1)} async-done(((bf16[512,1600]{1,0:T(8,128)(2,1)}), bf16[128,1600]{1,0:T(8,128)(2,1)}) %reduce-scatter.22.cloned.1.call-update) | async-done | bytes 409616 | tf_op jit(solution)/shard_map/reduce_scatter | solution.py:612
  441.8 18.1 %all_to_all.38 = bf16[128,8,256]{2,0,1:T(8,128)(2,1)S(1)} all-to-all(bf16[128,8,256]{2,0,1:T(8,128)(2,1)S(1)} %copy.115), channel_id=1, replica_groups=mesh['fsdp'=4,'z'=4,'core'=2] {'z','core'}, dimensions={1} | all-to-all | bytes 1048576 | tf_op jit(solution)/shard_map/all_to_all | solution.py:634
  461.3 12.9 %attend_back.1 = bf16[1024,768]{1,0:T(8,128)(2,1)S(1)} custom-call(bf16[1024,768]{1,0:T(8,128)(2,1)S(1)} %copy-done.2, s32[1024,1]{1,0:T(8,128)S(1)} %copy-done, s32[1,1024]{1,0:T(1,128)S(1)} %copy-done.3, bf16[1024,256]{1,0:T(8,128)(2,1)S(1)} %copy-done.1, f32[4,1024]{1,0:T(4,128)S(1)} %copy-done.4, bf16[1024,256]{1,0:T(8,128)(2,1)S(1)} %bitcast.116), custom_call_target="tpu_custom_call" | custom-call | tf_op jit(solution)/shard_map/attend_back/pallas_call | solution.py:121
  479.2 6.4 copy.123
  495.0 7.5 convolution_convert_fusion
  515.6 8.1 convolution_convert_fusion.1
  523.7 7.0 broadcast_in_dim.57
  530.7 47.6 %dynamic_update_slice.15 = bf16[6400,1600]{0,1:T(8,128)(2,1)} dynamic-update-slice(bf16[6400,1600]{0,1:T(8,128)(2,1)} %broadcast_in_dim.57, bf16[1600,1600]{0,1:T(8,128)(2,1)} %convolution_convert_fusion.1, s32[]{:T(128)S(6)} %select_n.96, s32[]{:T(128)} %constant.149.clone.1) | dynamic-update-slice | bytes 10240004 | tf_op jit(solution)/shard_map/dynamic_update_slice | solution.py:622
  578.3 30.8 %copy.130 = bf16[6400,1600]{1,0:T(8,128)(2,1)} copy(bf16[6400,1600]{0,1:T(8,128)(2,1)} %dynamic_update_slice.15) | data formatting | bytes 40960000
  617.8 38.1 %reduce-scatter.28.cloned.1.call-done = bf16[400,768]{1,0:T(8,128)(2,1)} async-done(((bf16[1600,768]{1,0:T(8,128)(2,1)}), bf16[400,768]{1,0:T(8,128)(2,1)}) %reduce-scatter.28.cloned.1.call-update) | async-done | bytes 614416 | tf_op jit(solution)/shard_map/reduce_scatter | solution.py:644
  667.1 10.4 copy.132
  677.7 173.6 %reduce-scatter.36.cloned.1.call-done = bf16[1600,1600]{1,0:T(8,128)(2,1)} async-done(((bf16[6400,1600]{1,0:T(8,128)(2,1)}), bf16[1600,1600]{1,0:T(8,128)(2,1)}) %reduce-scatter.36.cloned.1.call-update) | async-done | bytes 5120016
  851.3 9.5 copy.131
  865.9 37.7 %all-reduce.11.cloned.1.call-done = f32[8,2400]{1,0:T(8,128)} async-done(((f32[8,2400]{1,0:T(8,128)}), f32[8,2400]{1,0:T(8,128)}) %all-reduce.11.cloned.1.call-update) | async-done | bytes 76816
  905.2 10.2 psum.7
  916.7 72.4 %all-reduce.13.cloned.1.call-done = bf16[1600,800]{0,1:T(8,128)(2,1)} async-done(((bf16[1600,800]{0,1:T(8,128)(2,1)}), bf16[1600,800]{0,1:T(8,128)(2,1)}) %all-reduce.13.cloned.1.call-update) | async-done | bytes 2560016
  992.2 27.1 %reduce-scatter.34.cloned.1.call-done = bf16[400,200]{1,0:T(8,128)(2,1)} async-done(((bf16[1600,200]{1,0:T(8,128)(2,1)}), bf16[400,200]{1,0:T(8,128)(2,1)}) %reduce-scatter.34.cloned.1.call-update) | async-done | bytes 160016
  1021.3 57.3 %reduce-scatter.32.cloned.1.call-done = bf16[600,400]{1,0:T(8,128)(2,1)} async-done(((bf16[4800,400]{1,0:T(8,128)(2,1)}), bf16[600,400]{1,0:T(8,128)(2,1)}) %reduce-scatter.32.cloned.1.call-update) | async-done | bytes 480016
  1081.0 59.4 %reduce-scatter.40.cloned.1.call-done = bf16[1600,200]{0,1:T(8,128)(2,1)} async-done(((bf16[1600,1600]{0,1:T(8,128)(2,1)}), bf16[1600,200]{0,1:T(8,128)(2,1)}) %reduce-scatter.40.cloned.1.call-update) | async-done | bytes 640016
  (217 shorter events, 127.9 us)
Async XLA Ops:
  7.2 36.2 %copy-start.19 = (s32[8,128]{1,0:T(8,128)S(1)}, s32[8,128]{1,0:T(8,128)}, u32[]{:S(2)}) copy-start(s32[8,128]{1,0:T(8,128)} %constant.147.clone.1) | copy-start | bytes 12292
  7.2 34.9 %copy-start.28 = (bf16[200]{0:T(256)(128)(2,1)S(1)}, bf16[200]{0:T(256)(128)(2,1)}, u32[]{:S(2)}) copy-start(bf16[200]{0:T(256)(128)(2,1)} %param.33) | copy-start | bytes 1204
  7.2 34.9 %copy-start.20 = (bf16[800]{0:T(1024)(128)(2,1)S(1)}, bf16[800]{0:T(1024)(128)(2,1)}, u32[]{:S(2)}) copy-start(bf16[800]{0:T(1024)(128)(2,1)} %param.31) | copy-start | bytes 4804
  7.2 34.9 %copy-start.27 = (bf16[200]{0:T(256)(128)(2,1)S(1)}, bf16[200]{0:T(256)(128)(2,1)}, u32[]{:S(2)}) copy-start(bf16[200]{0:T(256)(128)(2,1)} %param.29) | copy-start | bytes 1204
  7.2 34.9 %copy-start.26 = (bf16[200]{0:T(256)(128)(2,1)S(1)}, bf16[200]{0:T(256)(128)(2,1)}, u32[]{:S(2)}) copy-start(bf16[200]{0:T(256)(128)(2,1)} %param.28) | copy-start | bytes 1204
  7.2 34.9 %copy-start.25 = (bf16[200]{0:T(256)(128)(2,1)S(1)}, bf16[200]{0:T(256)(128)(2,1)}, u32[]{:S(2)}) copy-start(bf16[200]{0:T(256)(128)(2,1)} %param.27) | copy-start | bytes 1204
  7.2 34.9 %copy-start.24 = (bf16[200]{0:T(256)(128)(2,1)S(1)}, bf16[200]{0:T(256)(128)(2,1)}, u32[]{:S(2)}) copy-start(bf16[200]{0:T(256)(128)(2,1)} %param.25) | copy-start | bytes 1204
  7.3 34.9 %copy-start.23 = (bf16[200]{0:T(256)(128)(2,1)S(1)}, bf16[200]{0:T(256)(128)(2,1)}, u32[]{:S(2)}) copy-start(bf16[200]{0:T(256)(128)(2,1)} %param.24) | copy-start | bytes 1204
  7.3 34.9 %copy-start.22 = (bf16[200]{0:T(256)(128)(2,1)S(1)}, bf16[200]{0:T(256)(128)(2,1)}, u32[]{:S(2)}) copy-start(bf16[200]{0:T(256)(128)(2,1)} %param.22) | copy-start | bytes 1204
  7.3 35.1 %copy-start.16 = (bf16[1,128,1600]{1,2,0:T(8,128)(2,1)S(1)}, bf16[1,128,1600]{1,2,0:T(8,128)(2,1)}, u32[]{:S(2)}) copy-start(bf16[1,128,1600]{1,2,0:T(8,128)(2,1)} %param.18) | copy-start | bytes 1228804
  7.3 31.2 %all-gather.12.cloned.1.call-start = ((), (), s32[]{:S(2)}) async-start(), calls=%async_computation.12 | async-start | bytes 1843200 | tf_op jit(solution)/shard_map/all_gather | solution.py:589
  9.2 144.2 %all-gather.18.cloned.1.call-start = ((), (), s32[]{:S(2)}) async-start(), calls=%async_computation.15 | async-start | bytes 3584000 | tf_op jit(solution)/shard_map/all_gather | solution.py:591
  10.0 170.9 %all-gather.14.cloned.1.call-start = ((), (), s32[]{:S(2)}) async-start(), calls=%async_computation.13 | async-start | bytes 6656000 | tf_op jit(solution)/shard_map/all_gather | solution.py:588
  42.0 185.6 %all-gather.22.cloned.1.call-start = ((), (), s32[]{:S(2)}) async-start(), calls=%async_computation.22 | async-start | bytes 4096000 | tf_op jit(solution)/shard_map/all_gather | solution.py:594
  153.1 91.3 %all-gather.20.cloned.1.call-start = ((), (), s32[]{:S(2)}) async-start(), calls=%async_computation.16 | async-start | bytes 7987200 | tf_op jit(solution)/shard_map/all_gather | solution.py:592
  159.6 18.8 %all-to-all-start = ((bf16[8,128,256]{1,2,0:T(8,128)(2,1)}), bf16[8,128,256]{1,2,0:T(8,128)(2,1)S(1)}, u32[]{:S(2)}, u32[]{:S(2)}) async-start(bf16[8,128,256]{1,2,0:T(8,128)(2,1)} %copy.107), calls=%async_computation | async-start | bytes 1048576 | tf_op jit(solution)/shard_map/all_to_all | solution.py:599
  163.1 123.7 %all-gather.16.cloned.1.call-start = ((), (), s32[]{:S(2)}) async-start(), calls=%async_computation.14 | async-start | bytes 2129920 | tf_op jit(solution)/shard_map/all_gather | solution.py:604
  185.7 140.3 %all-gather.26.cloned.1.call-start = ((), (), s32[]{:S(2)}) async-start(), calls=%async_computation.24 | async-start | bytes 2048000 | tf_op jit(solution)/shard_map/all_gather | solution.py:605
  186.5 154.7 %all-gather.24.cloned.1.call-start = ((), (), s32[]{:S(2)}) async-start(), calls=%async_computation.23 | async-start | bytes 7987200 | tf_op jit(solution)/shard_map/all_gather | solution.py:596
  232.2 164.0 %reduce-scatter.24.cloned.1.call-start = ((), (), s32[]{:S(2)}) async-start(), calls=%async_computation.18 | async-start | bytes 2129920 | tf_op jit(solution)/shard_map/reduce_scatter | solution.py:614
  357.6 77.2 %reduce-scatter.22.cloned.1.call-start = ((), (), s32[]{:S(2)}) async-start(), calls=%async_computation.17 | async-start | bytes 2129920 | tf_op jit(solution)/shard_map/reduce_scatter | solution.py:612
  367.4 244.5 %reduce-scatter.26.cloned.1.call-start = ((), (), s32[]{:S(2)}) async-start(), calls=%async_computation.19 | async-start | bytes 3833856 | tf_op jit(solution)/shard_map/reduce_scatter | solution.py:638
  368.7 72.9 %copy-start.10 = (bf16[1,128,1600]{2,1,0:T(8,128)(2,1)}, bf16[1,128,1600]{2,1,0:T(8,128)(2,1)S(1)}, u32[]{:S(2)}) copy-start(bf16[1,128,1600]{2,1,0:T(8,128)(2,1)S(1)} %copy.113) | copy-start | bytes 1228804
  495.0 119.5 %reduce-scatter.30.cloned.1.call-start = ((), (), s32[]{:S(2)}) async-start(), calls=%async_computation.21 | async-start | bytes 7987200 | tf_op jit(solution)/shard_map/reduce_scatter | solution.py:616
  502.5 112.9 %reduce-scatter.38.cloned.1.call-start = ((), (), s32[]{:S(2)}) async-start(), calls=%async_computation.30 | async-start | bytes 5990400
  507.7 148.1 %reduce-scatter.28.cloned.1.call-start = ((), (), s32[]{:S(2)}) async-start(), calls=%async_computation.20 | async-start | bytes 3072000 | tf_op jit(solution)/shard_map/reduce_scatter | solution.py:644
  515.2 336.2 %reduce-scatter.36.cloned.1.call-start = ((), (), s32[]{:S(2)}) async-start(), calls=%async_computation.27 | async-start | bytes 26624000
  609.1 294.6 %all-reduce.11.cloned.1.call-start = ((), (), s32[]{:S(2)}) async-start(), calls=%async_computation.28 | async-start | bytes 155648
  614.4 374.7 %all-reduce.13.cloned.1.call-start = ((), (), s32[]{:S(2)}) async-start(), calls=%async_computation.29 | async-start | bytes 5324800
  615.0 404.3 %reduce-scatter.34.cloned.1.call-start = ((), (), s32[]{:S(2)}) async-start(), calls=%async_computation.26 | async-start | bytes 1024000
  617.7 460.9 %reduce-scatter.32.cloned.1.call-start = ((), (), s32[]{:S(2)}) async-start(), calls=%async_computation.25 | async-start | bytes 5529600
  677.5 462.9 %reduce-scatter.40.cloned.1.call-start = ((), (), s32[]{:S(2)}) async-start(), calls=%async_computation.31 | async-start | bytes 5990400
  (23 other events, 247.4 us)
Sparse Core Ops, SparseCore 0:
  10.3 28.1 all-gather.11
  40.3 72.1 all-gather.17
  114.9 65.8 all-gather.13
  182.5 45.0 all-gather.21
  229.0 15.3 all-gather.19
  246.4 40.3 all-gather.15
  288.4 37.6 all-gather.25
  327.6 13.5 all-gather.23
  357.7 38.4 reduce-scatter.23
  398.4 36.3 reduce-scatter.21
  495.1 41.2 reduce-scatter.25
  538.5 11.9 reduce-scatter.29
  553.0 62.3 reduce-scatter.37
  618.6 37.1 reduce-scatter.27
  659.1 192.1 reduce-scatter.35
  854.1 49.4 all-reduce.10
  906.9 82.0 all-reduce.12
  992.7 26.5 reduce-scatter.33
  1021.7 56.8 reduce-scatter.31
  1080.9 59.5 reduce-scatter.39

commit v2 on v1

v2 whole, which is shorter than its diff:
```python
from functools import partial
import math

import jax
import jax.numpy as jnp
from jax import lax
from jax.experimental import pallas as pl
from jax.experimental.pallas import tpu as pltpu
from jax.sharding import Mesh
from jax.sharding import PartitionSpec as P

HD = 64
EPS = 1e-05
FLOOR = -1e30
BF = jnp.bfloat16
F32 = jnp.float32
CTX = ("z", "core")
MESH = pl.DeviceIdType.MESH
VMEM = pl.BlockSpec(memory_space=pltpu.VMEM)
HBM = pl.BlockSpec(memory_space=pl.ANY)
GELU_A = math.sqrt(2.0 / math.pi)
GELU_B = 0.044715


def up(n):
    return -(-n // 128) * 128


def sems(*counts):
    return [pltpu.SemaphoreType.DMA(c if isinstance(c, tuple) else (c,)) for c in counts]


def shape(dims, kind=BF):
    return jax.ShapeDtypeStruct(dims, kind)


def dot(a, b):
    return jnp.dot(a, b, preferred_element_type=F32)


def dot_nt(a, b):
    return lax.dot_general(a, b, (((1,), (1,)), ((), ())), preferred_element_type=F32)


def dot_tn(a, b):
    return lax.dot_general(a, b, (((0,), (0,)), ((), ())), preferred_element_type=F32)


def norm_rows(rows):
    centred = rows - jnp.mean(rows, axis=-1, keepdims=True)
    rstd = lax.rsqrt(jnp.mean(centred * centred, axis=-1, keepdims=True) + EPS)
    return centred * rstd, rstd


def norm_back(upstream, xhat, rstd, gain):
    inner = upstream * gain
    return rstd * (
        inner
        - jnp.mean(inner, axis=-1, keepdims=True)
        - xhat * jnp.mean(inner * xhat, axis=-1, keepdims=True)
    )


def gelu_pair(v):
    sq = v * v
    t = jnp.tanh(GELU_A * v * (1.0 + GELU_B * sq))
    half = 0.5 * (1.0 + t)
    slope = half + 0.5 * v * (1.0 - t * t) * (GELU_A * (1.0 + 3.0 * GELU_B * sq))
    return v * half, slope


def positions(order_table, rows):
    block = rows // order_table.shape[0]
    return (order_table[:, None] * block + jnp.arange(block, dtype=jnp.int32)[None]).reshape(rows)


def remote(src, dst, send, recv, **to):
    return pltpu.make_async_remote_copy(
        src_ref=src, dst_ref=dst, send_sem=send, recv_sem=recv, device_id=to, device_id_type=MESH
    )


def column_segments(ranks, d, width, grain):
    own = 3 * d // ranks
    runs = []
    for src in range(ranks):
        for part in range(3):
            for dst in range(ranks):
                low = part * d + dst * width
                first = max(src * own, low)
                last = min((src + 1) * own, low + width, (part + 1) * d)
                if first < last:
                    at = part * width + first - low
                    runs.append(
                        (src, (first - src * own) // grain, dst, at // grain, (last - first) // grain)
                    )
    return runs


def meet(peers):
    barrier = pltpu.get_barrier_semaphore()
    for peer in peers:
        pl.semaphore_signal(barrier, inc=1, device_id=peer, device_id_type=MESH)
    pl.semaphore_wait(barrier, len(peers))


class Line:
    def __init__(self, at, size, sems):
        self.at, self.size = at, size
        self.right, self.left, self.recv = sems
        self.z = lax.axis_index("z")

    def copy(self, block, way):
        send = (self.right if way > 0 else self.left).at[block]
        at = self.at(block)
        return remote(at, at, send, self.recv.at[block], z=self.z + way)

    def start(self):
        @pl.when(self.z < self.size - 1)
        def _():
            self.copy(self.z, 1).start()

        @pl.when(self.z > 0)
        def _():
            self.copy(self.z, -1).start()

    def step(self, s, then=None):
        @pl.when(self.z >= s)
        def _():
            block = self.z - s
            self.copy(block, 1).wait_recv()

            @pl.when(self.z < self.size - 1)
            def _():
                self.copy(block, 1).start()

            if then is not None:
                then(block)

        @pl.when(self.z + s < self.size)
        def _():
            block = self.z + s
            self.copy(block, -1).wait_recv()

            @pl.when(self.z > 0)
            def _():
                self.copy(block, -1).start()

            if then is not None:
                then(block)

    def finish(self):
        for s in range(self.size):

            @pl.when((self.z >= s) & (self.z < self.size - 1))
            def _():
                self.copy(self.z - s, 1).wait_send()

            @pl.when((self.z + s < self.size) & (self.z > 0))
            def _():
                self.copy(self.z + s, -1).wait_send()


class LineSum:
    def __init__(self, parts, from_left, from_right, size, sems):
        self.parts, self.ins, self.size = parts, (from_left, from_right), size
        self.send, self.recv_left, self.recv_right = sems
        self.z = lax.axis_index("z")

    def copy(self, block, way):
        recv = self.recv_left if way > 0 else self.recv_right
        there = self.ins[0 if way > 0 else 1].at[block]
        return remote(
            self.parts.at[block], there, self.send.at[block], recv.at[block], z=self.z + way
        )

    def first(self):
        for way, edge in ((1, 0), (-1, self.size - 1)):

            @pl.when(self.z == edge)
            def _():
                for hop in range(self.size - 1, 0, -1):
                    self.copy(self.z + way * hop, way).start()

    def add_on(self, block, way):
        self.copy(block, way).wait_recv()
        came = self.ins[0 if way > 0 else 1]
        self.parts[block] = (
            self.parts[block].astype(F32) + came[block].astype(F32)
        ).astype(self.parts.dtype)
        self.copy(block, way).start()

    def step(self, s):
        right, left = self.z + self.size - 1 - s, s - (self.size - 1 - self.z)

        @pl.when((self.z > 0) & (right < self.size) & (right > self.z))
        def _():
            self.add_on(right, 1)

        @pl.when((self.z < self.size - 1) & (left >= 0) & (left < self.z))
        def _():
            self.add_on(left, -1)

    def finish(self):
        @pl.when(self.z > 0)
        def _():
            self.copy(self.z, 1).wait_recv()

        @pl.when(self.z == 0)
        def _():
            self.ins[0][self.z] = jnp.zeros(self.parts.shape[1:], self.parts.dtype)

        @pl.when(self.z < self.size - 1)
        def _():
            self.copy(self.z, -1).wait_recv()

        @pl.when(self.z == self.size - 1)
        def _():
            self.ins[1][self.z] = jnp.zeros(self.parts.shape[1:], self.parts.dtype)

    def sent(self):
        for block in range(self.size):

            @pl.when(self.z < block)
            def _():
                self.copy(block, 1).wait_send()

            @pl.when(self.z > block)
            def _():
                self.copy(block, -1).wait_send()


def halves(n):
    return ((0, n // 2), (n // 2, n - n // 2))


class Plane:
    def __init__(self, size):
        self.size, self.f = size, lax.axis_index("fsdp")
        self.square = size == 4
        f = self.f
        self.peers = [lax.rem(f + i, size) for i in range(1, size)]
        if self.square:
            self.x, self.y, self.far = f + 1 - 2 * lax.rem(f, 2), lax.rem(f + 2, 4), 3 - f
            self.peers = [self.x, self.y, self.far]


class PlaneGather:
    def __init__(self, plane, at, sems):
        self.p, self.at = plane, at
        self.send, self.recv = sems
        f = plane.f
        if plane.square:
            x, y = plane.x, plane.y
            self.early = [(f, 0, x), (f, 1, y), (f, 0, y), (f, 1, x)]
            self.late = [(x, 0, y), (y, 1, x)]
        else:
            self.early = [(f, h, g) for g in plane.peers for h in range(2)]
            self.late = []

    def copy(self, n, move):
        g, half, to = move
        at = self.at(g, half)
        return remote(at, at, self.send.at[n], self.recv.at[g, half], fsdp=to)

    def arrive(self, g, half):
        at = self.at(g, half)
        remote(at, at, self.send.at[0], self.recv.at[g, half], fsdp=g).wait_recv()

    def start(self):
        for n, move in enumerate(self.early):
            self.copy(n, move).start()

    def mid(self):
        for n, move in enumerate(self.late):
            self.arrive(move[0], move[1])
            self.copy(len(self.early) + n, move).start()

    def end(self):
        known = [(m[0], m[1]) for m in self.late]
        for g in self.p.peers:
            for half in range(2):
                if not any(g is a and half == b for a, b in known):
                    self.arrive(g, half)

    def sent(self):
        for n, move in enumerate(self.early + self.late):
            self.copy(n, move).wait_send()


class PlaneSum:
    def __init__(self, plane, at, came, sems):
        self.p, self.at, self.came = plane, at, came
        self.send, self.recv = sems
        if plane.square:
            x, y, far = plane.x, plane.y, plane.far
            self.early = [(far, 0, x, 0), (far, 1, y, 1), (x, 0, x, 2), (y, 1, y, 3)]
            self.late = [(y, 0, y, 4), (x, 1, x, 5)]
            self.mine = [[2, 4], [3, 5]]
        else:
            n = plane.size
            self.early = [
                (g, h, g, 2 * i + h) for i, g in enumerate(plane.peers) for h in range(2)
            ]
            self.late = []
            self.mine = [[2 * i + h for i in range(n - 1)] for h in range(2)]

    def copy(self, move):
        g, half, to, slot = move
        return remote(
            self.at(g, half), self.came(slot, half), self.send.at[slot], self.recv.at[slot], fsdp=to
        )

    def arrive(self, slot, half):
        there = self.came(slot, half)
        remote(
            there, there, self.send.at[slot], self.recv.at[slot], fsdp=self.p.peers[0]
        ).wait_recv()

    def start(self):
        for move in self.early:
            self.copy(move).start()

    def mid(self):
        for slot, move in enumerate(self.late):
            self.arrive(slot, move[1])
            at, came = self.at(move[0], move[1]), self.came(slot, move[1])
            at[...] = (at[...].astype(F32) + came[...].astype(F32)).astype(at.dtype)
            self.copy(move).start()

    def end(self):
        for half in range(2):
            for slot in self.mine[half]:
                self.arrive(slot, half)

    def total(self, half):
        out = self.at(self.p.f, half)[...].astype(F32)
        for slot in self.mine[half]:
            out += self.came(slot, half)[...].astype(F32)
        return out

    def sent(self):
        for move in self.early + self.late:
            self.copy(move).wait_send()


def query_block(length):
    return max(128, min(256, length, 256 * 1024 // length))


def attend_head(h, width, q_block, qkv, pos_col, pos_row, out, lse):
    rows = qkv.shape[0]
    k = qkv[:, width + h * HD : width + (h + 1) * HD]
    v = qkv[:, 2 * width + h * HD : 2 * width + (h + 1) * HD]
    for b in range(rows // q_block):
        at = slice(b * q_block, (b + 1) * q_block)
        q = qkv[at, h * HD : (h + 1) * HD] * BF(HD**-0.5)
        s = dot_nt(k, q)
        s = jnp.where(pos_col[...] <= pos_row[:, at], s, FLOOR)
        top = jnp.max(s, axis=0, keepdims=True)
        p = jnp.exp(s - top)
        total = jnp.sum(p, axis=0, keepdims=True)
        o = dot_tn(v, p.astype(BF)) * (1.0 / total)
        out[at, h * HD : (h + 1) * HD] = o.T.astype(BF)
        lse[h : h + 1, at] = top + jnp.log(total)


def attend_back_head(h, width, q_block, qkv, pos_col, pos_row, out, lse, dout, dqkv, acc):
    rows = qkv.shape[0]
    k = qkv[:, width + h * HD : width + (h + 1) * HD]
    v = qkv[:, 2 * width + h * HD : 2 * width + (h + 1) * HD]
    for b in range(rows // q_block):
        at = slice(b * q_block, (b + 1) * q_block)
        q = qkv[at, h * HD : (h + 1) * HD] * BF(HD**-0.5)
        do = dout[at, h * HD : (h + 1) * HD]
        o = out[at, h * HD : (h + 1) * HD]
        delta = jnp.sum(do.astype(F32).T * o.astype(F32).T, axis=0, keepdims=True)
        s = dot_nt(k, q)
        p = jnp.where(pos_col[...] <= pos_row[:, at], jnp.exp(s - lse[h : h + 1, at]), 0.0)
        dp = dot_nt(v, do)
        ds = (p * (dp - delta)).astype(BF)
        dq = dot_tn(k, ds) * (HD**-0.5)
        dqkv[at, h * HD : (h + 1) * HD] = dq.T.astype(BF)
        dk = dot(ds, q)
        dv = dot(p.astype(BF), do)
        if b == 0:
            acc[:, :HD] = dk
            acc[:, HD:] = dv
        else:
            acc[:, :HD] += dk
            acc[:, HD:] += dv
    dqkv[:, width + h * HD : width + (h + 1) * HD] = acc[:, :HD].astype(BF)
    dqkv[:, 2 * width + h * HD : 2 * width + (h + 1) * HD] = acc[:, HD:].astype(BF)


def start_kernel(
    cfg,
    tok,
    wq,
    small,
    pj,
    ot,
    pos_col,
    pos_row,
    h1,
    w,
    qkv,
    att,
    lse,
    smalls,
    p1,
    o_all,
    a_own,
    toks,
    vecs,
    small_send,
    small_recv,
    q_send,
    q_recv,
    q_local,
    x_send,
    x_recv,
    t_right,
    t_left,
    t_recv,
    c_send,
    c_recv,
    p1_send,
    p1_recv,
    p_local,
    a_send,
    a_recv,
    o_right,
    o_left,
    o_recv,
    ox_send,
    ox_recv,
    oc_send,
    oc_recv,
):
    fs, nz, d, heads = cfg
    cs = 2 * nz
    f, z, core = lax.axis_index("fsdp"), lax.axis_index("z"), lax.axis_index("core")
    rank = 2 * z + core
    rows, lanes = tok.shape[0], wq.shape[2]
    width = heads * HD
    grain = wq.shape[1]
    own_rows = d // fs
    part = d // cs
    lanes_of = lambda g: pl.ds(pl.multiple_of(g * lanes, 128), lanes)
    runs = column_segments(cs, d, width, grain)
    plane = Plane(fs)
    planes = plane.peers

    w[:, :, lanes_of(f)] = jnp.zeros((w.shape[0], grain, lanes), BF)
    own_out = o_all.at[rank, :, :, lanes_of(f)]
    pltpu.sync_copy(ot, own_out)
    ranks = [lax.rem(rank + i, cs) for i in range(1, cs)]
    meet([dict(z=r // 2, core=lax.rem(r, 2)) for r in ranks] + [dict(fsdp=p) for p in planes])

    def run_copy(n):
        src, first, dst, at, count = runs[n]
        here, there = wq.at[pl.ds(first, count)], w.at[pl.ds(at, count), :, lanes_of(f)]
        if src == dst:
            return pltpu.make_async_copy(here, there, q_local.at[n])
        return remote(here, there, q_send.at[n], q_recv.at[n], z=dst // 2, core=dst % 2)

    for n, run in enumerate(runs):

        @pl.when(rank == run[0])
        def _():
            run_copy(n).start()

    def small_copy(i):
        r = ranks[i]
        to = smalls.at[rank]
        return remote(small, to, small_send.at[i], small_recv.at[rank], z=r // 2, core=lax.rem(r, 2))

    for i in range(cs - 1):
        small_copy(i).start()

    share = p1.shape[1]

    def p1_copy(i):
        here = pj.at[pl.ds(planes[i] * share, share)]
        return remote(here, p1.at[f], p1_send.at[i], p1_recv.at[f], fsdp=planes[i])

    p1_local = pltpu.make_async_copy(pj.at[pl.ds(f * share, share)], p1.at[f], p_local.at[0])
    p1_local.start()
    for i in range(fs - 1):
        p1_copy(i).start()

    def ox_copy(i, block):
        at = o_all.at[2 * block + core, :, :, lanes_of(f)]
        return remote(at, at, ox_send.at[i, block], ox_recv.at[f, block], fsdp=planes[i])

    def ox_arrival(g, block):
        at = o_all.at[2 * block + core, :, :, lanes_of(g)]
        return remote(at, at, ox_send.at[0, block], ox_recv.at[g, block], fsdp=g)

    def oc_copy(g, block):
        at = o_all.at[2 * block + core, :, :, lanes_of(g)]
        return remote(at, at, oc_send.at[g, block], oc_recv.at[g, block], core=1 - core)

    def oc_arrival(g, block):
        at = o_all.at[2 * block + 1 - core, :, :, lanes_of(g)]
        return remote(at, at, oc_send.at[g, block], oc_recv.at[g, block], core=1 - core)

    def out_block(block):
        for i in range(fs - 1):
            ox_copy(i, block).start()
        oc_copy(f, block).start()

    out_block(z)

    for n, run in enumerate(runs):

        @pl.when(rank == run[2])
        def _():
            if run[0] == run[2]:
                run_copy(n).wait()
            else:
                run_copy(n).wait_recv()

    gather = PlaneGather(
        plane, lambda g, h: w.at[pl.ds(*halves(w.shape[0])[h]), :, lanes_of(g)], (x_send, x_recv)
    )
    gather.start()

    pltpu.sync_copy(tok, toks.at[rank])
    line = Line(lambda b: toks.at[2 * b + core], nz, (t_right, t_left, t_recv))

    def pass_on(block):
        at = toks.at[2 * block + core]
        return remote(at, at, c_send.at[block], c_recv.at[block], core=1 - core)

    def arrival(block):
        at = toks.at[2 * block + 1 - core]
        return remote(at, at, c_send.at[block], c_recv.at[block], core=1 - core)

    line.start()
    pass_on(z).start()

    smalls[rank] = small[...]
    vecs[...] = jnp.zeros(vecs.shape, F32)
    for i in range(1, cs):
        back = lax.rem(rank + cs - i, cs)
        remote(small, smalls.at[back], small_send.at[i - 1], small_recv.at[back], z=z).wait_recv()
    for r in range(cs):
        vecs[:, part * r : part * (r + 1)] = smalls[r, 0:8, 0:part]
    for g in range(fs):
        h1[:, lanes * g + own_rows : lanes * (g + 1)] = jnp.zeros(
            (h1.shape[0], lanes - own_rows), BF
        )

    for s in range(1, nz):
        line.step(s, lambda b: pass_on(b).start())

    out_line = Line(
        lambda b: o_all.at[2 * b + core, :, :, lanes_of(f)], nz, (o_right, o_left, o_recv)
    )
    out_line.start()
    gather.mid()
    for b in range(nz):
        arrival(b).wait_recv()

    step = min(32, rows)

    def norm_chunk(i, _):
        block, at = i // (rows // step), lax.rem(i, rows // step) * step
        xhat, _ = norm_rows(toks[block, pl.ds(at, step), :].astype(F32))
        h = (xhat * vecs[0:1, 0:d] + vecs[1:2, 0:d]).astype(BF)
        to = pl.ds(pl.multiple_of(i * step, step), step)
        for g in range(fs):
            h1[to, lanes * g : lanes * g + own_rows] = h[:, own_rows * g : own_rows * (g + 1)]
        return 0

    lax.fori_loop(0, cs * rows // step, norm_chunk, 0)
    out_line.step(1, out_block)
    gather.end()

    tall = min(256, cs * rows)
    head_lanes = pl.ds(pl.multiple_of(rank * width, 128), width)

    def project(i, _):
        at = pl.ds(pl.multiple_of(i * tall, tall), tall)
        full = dot_nt(h1[at, :], w[...].reshape(3 * width, fs * lanes))
        qkv[at, 0:width] = (full[:, 0:width] + vecs[2:3, head_lanes]).astype(BF)
        qkv[at, width : 2 * width] = full[:, width : 2 * width].astype(BF)
        qkv[at, 2 * width :] = (full[:, 2 * width :] + vecs[3:4, head_lanes]).astype(BF)
        return 0

    lax.fori_loop(0, cs * rows // tall, project, 0)
    for s in range(2, nz):
        out_line.step(s, out_block)
    for h in range(heads):
        attend_head(h, width, query_block(cs * rows), qkv, pos_col, pos_row, att, lse)

    def a_copy(i):
        r = ranks[i]
        here = att.at[pl.ds(pl.multiple_of(r * rows, rows), rows)]
        there = a_own.at[:, head_lanes]
        return remote(here, there, a_send.at[i], a_recv.at[rank], z=r // 2, core=lax.rem(r, 2))

    for i in range(cs - 1):
        a_copy(i).start()
    a_own[:, head_lanes] = att[pl.ds(pl.multiple_of(rank * rows, rows), rows), :]

    for g in planes:
        for b in range(nz):
            ox_arrival(g, b).wait_recv()
            oc_copy(g, b).start()
    for i in range(1, cs):
        back = lax.rem(rank + cs - i, cs)
        to = a_own.at[:, pl.ds(pl.multiple_of(back * width, 128), width)]
        remote(to, to, a_send.at[0], a_recv.at[back], z=z).wait_recv()
    p1_local.wait()
    for g in planes:
        remote(p1.at[g], p1.at[g], p1_send.at[0], p1_recv.at[g], fsdp=g).wait_recv()
    for g in range(fs):
        for b in range(nz):
            oc_arrival(g, b).wait_recv()

    for n, run in enumerate(runs):
        if run[0] != run[2]:

            @pl.when(rank == run[0])
            def _():
                run_copy(n).wait_send()

    for i in range(cs - 1):
        small_copy(i).wait_send()
        a_copy(i).wait_send()
    gather.sent()
    for i in range(fs - 1):
        p1_copy(i).wait_send()
        for b in range(nz):
            ox_copy(i, b).wait_send()
    for g in range(fs):
        for b in range(nz):
            oc_copy(g, b).wait_send()
    line.finish()
    out_line.finish()
    for b in range(nz):
        pass_on(b).wait_send()


def start(cfg, tok, wq, small, pj, ot, pos):
    fs, nz, d, heads = cfg
    cs = 2 * nz
    rows, lanes = tok.shape[0], wq.shape[2]
    width, length = heads * HD, rows * cs
    runs = len(column_segments(cs, d, width, wq.shape[1]))
    return pl.pallas_call(
        partial(start_kernel, cfg),
        out_shape=(
            shape((length, fs * lanes)),
            shape((3 * width // wq.shape[1], wq.shape[1], fs * lanes)),
            shape((length, 3 * width)),
            shape((length, width)),
            shape((heads, length), F32),
            shape((cs,) + small.shape, F32),
            shape((fs, pj.shape[0] // fs) + pj.shape[1:]),
            shape((cs,) + ot.shape[:2] + (fs * lanes,)),
            shape((rows, cs * width)),
        ),
        in_specs=[VMEM, VMEM, VMEM, HBM, HBM, VMEM, VMEM],
        out_specs=(VMEM, VMEM, VMEM, VMEM, VMEM, VMEM, HBM, HBM, VMEM),
        scratch_shapes=[
            pltpu.VMEM((cs, rows, d), BF),
            pltpu.VMEM((8, width * cs), F32),
        ]
        + sems(cs, cs, runs, runs, runs, 2 * fs, (fs, 2), nz, nz, nz, nz, nz, fs, fs, 1, cs, cs)
        + sems(nz, nz, nz, (fs, nz), (fs, nz), (fs, nz), (fs, nz)),
        name="start",
        compiler_params=pltpu.CompilerParams(
            collective_id=0, has_side_effects=True, vmem_limit_bytes=56 * 2**20
        ),
    )(tok, wq, small, pj, ot, pos[:, None], pos[None, :])


def middle_kernel(
    cfg,
    a_own,
    tok,
    ct,
    ct_split,
    vec,
    fb,
    o_all,
    p1,
    fc,
    middle,
    d_middle,
    d_att,
    out_part,
    fc_grad,
    p_sum,
    og,
    sums,
    a_pad,
    ov,
    fcv,
    pjv,
    p2,
    ctb,
    cto,
    h2b,
    actb,
    dbo,
    dbp,
    dh,
    in_left,
    in_right,
    own_dh,
    da,
    dsp,
    pg,
    pr,
    stage,
    local,
    p2_send,
    p2_recv,
    p3_send,
    p3_recv,
    pc_send,
    pc_recv,
    f_send,
    f_recv,
    fc_send,
    fc_recv,
    c_right,
    c_left,
    c_recv,
    h_right,
    h_left,
    h_recv,
    e_send,
    e_recv,
    r_send,
    r_left,
    r_right,
    d_send,
    d_recv,
    g_send,
    g_recv,
):
    fs, nz, d, heads = cfg
    cs = 2 * nz
    f, z, core = lax.axis_index("fsdp"), lax.axis_index("z"), lax.axis_index("core")
    rank = 2 * z + core
    rows = tok.shape[0]
    width = heads * HD
    lanes = o_all.shape[3] // fs
    own_rows, part = d // fs, d // cs
    share, grain = p1.shape[1], p1.shape[2]
    he, hf = ct_split.shape[1] // 2, fc.shape[2]
    slot = he // nz
    ff = 2 * hf
    fc_rows = fc.shape[0]
    tall = nz * rows
    step = min(32, rows)
    plane = Plane(fs)
    ranks = [lax.rem(rank + i, cs) for i in range(1, cs)]
    half_at = lambda k: pl.ds(pl.multiple_of(k * hf, 128), hf)
    e_at = lambda k: pl.ds(pl.multiple_of(k * he, 128), he)

    load_out = pltpu.make_async_copy(o_all, ov, local.at[0])
    fc_at = lambda g, k, h: fcv.at[
        pl.ds(g * fc_rows + halves(fc_rows)[h][0], halves(fc_rows)[h][1]), :, half_at(k)
    ]
    load_fc = [
        pltpu.make_async_copy(fc.at[pl.ds(*halves(fc_rows)[h])], fc_at(f, core, h), local.at[1 + h])
        for h in range(2)
    ]
    load_p2 = pltpu.make_async_copy(p1.at[z], p2.at[z], local.at[3])
    load_out.start()
    for copy in load_fc:
        copy.start()
    load_p2.start()
    meet(
        [dict(z=r // 2, core=lax.rem(r, 2)) for r in ranks] + [dict(fsdp=p) for p in plane.peers]
    )

    def swap(n, here, there):
        return remote(here, there, e_send.at[n], e_recv.at[n], core=1 - core)

    def p2_copy(i):
        to = lax.rem(z + i, nz)
        return remote(p1.at[to], p2.at[z], p2_send.at[to], p2_recv.at[z], z=to)

    for i in range(1, nz):
        p2_copy(i).start()

    for copy in load_fc:
        copy.wait()
    fc_gather = PlaneGather(plane, lambda g, h: fc_at(g, core, h), (f_send, f_recv))
    fc_gather.start()

    def fc_pass(g):
        at = fcv.at[pl.ds(g * fc_rows, fc_rows), :, half_at(core)]
        return remote(at, at, fc_send.at[g], fc_recv.at[g], core=1 - core)

    def fc_came(g):
        at = fcv.at[pl.ds(g * fc_rows, fc_rows), :, half_at(1 - core)]
        return remote(at, at, fc_send.at[g], fc_recv.at[g], core=1 - core)

    fc_pass(f).start()

    ctb[z] = ct_split[...]
    c_line = Line(lambda b: ctb.at[b], nz, (c_right, c_left, c_recv))
    c_line.start()

    for g in range(fs):
        a_pad[core, :, lanes * g : lanes * g + own_rows] = a_own[
            :, own_rows * g : own_rows * (g + 1)
        ]
        a_pad[core, :, lanes * g + own_rows : lanes * (g + 1)] = jnp.zeros(
            (rows, lanes - own_rows), BF
        )
    swap_a = swap(4, a_pad.at[core], a_pad.at[core])
    swap_a.start()
    load_out.wait()
    branch = dot_nt(a_pad[core], ov[...].reshape(d, fs * lanes))
    middle[...] = tok[...].astype(F32) + branch + vec[0:1, :]

    def norm_chunk(i, _):
        at = pl.ds(pl.multiple_of(i * step, step), step)
        xhat, _ = norm_rows(middle[at, :])
        h2b[core, z, at, :] = (xhat * vec[1:2, :] + vec[2:3, :]).astype(BF)
        return 0

    lax.fori_loop(0, rows // step, norm_chunk, 0)
    h_line = Line(lambda b: h2b.at[core, b], nz, (h_right, h_left, h_recv))
    h_line.start()
    c_line.step(1)
    fc_gather.mid()
    h_line.step(1)

    load_p2.wait()
    for i in range(1, nz):
        back = lax.rem(z + nz - i, nz)
        remote(p2.at[back], p2.at[back], p2_send.at[0], p2_recv.at[back], z=back).wait_recv()
    half_z = lambda h: pl.ds(*halves(nz)[h])
    pjv[core, :, f] = p2[...]
    p_gather = PlaneGather(plane, lambda g, h: pjv.at[core, half_z(h), g], (p3_send, p3_recv))
    p_gather.start()

    def p_pass(g):
        at = pjv.at[core, :, g]
        return remote(at, at, pc_send.at[g], pc_recv.at[g], core=1 - core)

    def p_came(g):
        at = pjv.at[1 - core, :, g]
        return remote(at, at, pc_send.at[g], pc_recv.at[g], core=1 - core)

    p_pass(f).start()
    for s in range(2, nz):
        c_line.step(s)
        h_line.step(s)
    swap_ct = swap(0, ctb.at[:, :, e_at(1 - core)], cto)
    swap_h2 = swap(1, h2b.at[core], h2b.at[core])
    swap_h2.start()
    swap_ct.start()
    fc_gather.end()
    for g in plane.peers:
        fc_pass(g).start()
    p_gather.mid()
    for g in range(fs):
        fc_came(g).wait_recv()
    p_gather.end()
    for g in plane.peers:
        p_pass(g).start()
    for g in range(fs):
        p_came(g).wait_recv()

    chunk = 256 if ff % 256 == 0 else 128

    def feed(i, _):
        at = pl.ds(pl.multiple_of(i * chunk, chunk), chunk)
        before = dot(h2b[core].reshape(tall, d), fcv[:, :, at].reshape(d, chunk)) + fb[:, at]
        act, slope = gelu_pair(before)
        actb[core, :, :, at] = act.astype(BF).reshape(nz, rows, chunk)
        back = dot(ctb[...].reshape(tall, 2 * he), pjv[:, :, :, :, :, at].reshape(2 * he, chunk))
        low = (back * slope).astype(BF)
        dbo[:, :, at] = low.reshape(nz, rows, chunk)
        sums[4:5, at] = jnp.sum(low.astype(F32), axis=0, keepdims=True)
        return 0

    lax.fori_loop(0, ff // chunk, feed, 0)
    swap_act = swap(2, actb.at[core], actb.at[core])
    swap_db = swap(3, dbo.at[:, :, half_at(1 - core)], dbp)
    swap_act.start()
    swap_db.start()

    def hidden_back(i, _):
        block = lax.rem(z + 1 + i, nz)
        part = dot_nt(dbo[block], fcv[...].reshape(d, ff))
        dh[block] = part.astype(BF)

        @pl.when(block == z)
        def _():
            own_dh[...] = part

        return 0

    lax.fori_loop(0, nz, hidden_back, 0)
    r_line = LineSum(dh, in_left, in_right, nz, (r_send, r_left, r_right))
    r_line.first()

    def output_part(k, i):
        w = pjv[k, i].reshape(slot, ff)
        part = dot_nt(actb[core].reshape(tall, ff), w)
        low = k * he + i * slot
        ctb[:, :, low : low + slot] = part.astype(BF).reshape(nz, rows, slot)

    swap_ct.wait_recv()
    swap_act.wait_recv()
    pieces = 2 if hf % 256 == 0 or ff % 512 else 4
    for low in range(0, ff, ff // pieces):
        cols = slice(low, low + ff // pieces)
        pg[:, :, :, :, cols] = (
            (
                dot_tn(
                    ctb[:, :, e_at(core)].reshape(tall, he),
                    actb[core, :, :, cols].reshape(tall, ff // pieces),
                )
                + dot_tn(
                    cto[...].reshape(tall, he),
                    actb[1 - core, :, :, cols].reshape(tall, ff // pieces),
                )
            )
            .astype(BF)
            .reshape(nz, fs, share, grain, ff // pieces)
        )
    p_total = PlaneSum(
        plane,
        lambda g, h: pg.at[half_z(h), g],
        lambda n, h: pr.at[n, pl.ds(0, halves(nz)[h][1])],
        (g_send, g_recv),
    )
    p_total.start()
    c_line.finish()
    swap_ct.wait_send()
    keep_out = pltpu.make_async_copy(ctb, out_part, local.at[6])
    for s in range(1, nz - 1):
        r_line.step(s)
        if s == 1:
            for k in range(2):
                for i in range(nz):
                    output_part(k, i)
            keep_out.start()
    swap_h2.wait_recv()
    swap_db.wait_recv()
    own_db = dbo[:, :, half_at(core)].reshape(tall, hf)
    other_db = dbp[...].reshape(tall, hf)
    cut = 512
    for low in range(0, d, cut):
        high = min(d, low + cut)
        fc_grad[low:high, :] = (
            dot_tn(h2b[core, :, :, low:high].reshape(tall, high - low), own_db)
            + dot_tn(h2b[1 - core, :, :, low:high].reshape(tall, high - low), other_db)
        ).astype(BF)
    p_total.mid()
    r_line.finish()

    sums[0:4, :] = jnp.zeros((4, sums.shape[1]), F32)
    dsp[core] = jnp.zeros(dsp.shape[1:], BF)

    def norm_back_chunk(i, _):
        at = pl.ds(pl.multiple_of(i * step, step), step)
        g = own_dh[at, :] + in_left[z, at, :].astype(F32) + in_right[z, at, :].astype(F32)
        xhat, rstd = norm_rows(middle[at, :])
        dm = ct[at, :].astype(F32) + norm_back(g, xhat, rstd, vec[1:2, :])
        low = dm.astype(BF)
        d_middle[at, :] = dm
        for c in range(cs):
            to = (c % 2) * he + (c // 2) * slot
            dsp[core, at, to : to + part] = low[:, c * part : (c + 1) * part]
        sums[0:1, 0:d] += jnp.sum(low.astype(F32), axis=0, keepdims=True)
        sums[1:2, 0:d] += jnp.sum(g * xhat, axis=0, keepdims=True)
        sums[2:3, 0:d] += jnp.sum(g, axis=0, keepdims=True)
        sums[3:4, 0:d] += jnp.sum(ct[at, :].astype(F32), axis=0, keepdims=True)
        return 0

    lax.fori_loop(0, rows // step, norm_back_chunk, 0)
    swap_d = swap(5, dsp.at[core], dsp.at[core])
    swap_d.start()
    back = dot(d_middle[...].astype(BF), ov[...].reshape(d, fs * lanes)).astype(BF)
    for g in range(fs):
        da[:, own_rows * g : own_rows * (g + 1)] = back[:, lanes * g : lanes * g + own_rows]
    if d < cs * width:
        da[:, d:] = jnp.zeros((rows, cs * width - d), BF)

    def d_copy(i):
        r = ranks[i]
        here = da.at[:, pl.ds(pl.multiple_of(r * width, 128), width)]
        there = d_att.at[pl.ds(pl.multiple_of(rank * rows, rows), rows)]
        return remote(here, there, d_send.at[i], d_recv.at[rank], z=r // 2, core=lax.rem(r, 2))

    for i in range(cs - 1):
        d_copy(i).start()
    d_att[pl.ds(pl.multiple_of(rank * rows, rows), rows), :] = da[
        :, pl.ds(pl.multiple_of(rank * width, 128), width)
    ]

    swap_a.wait_recv()
    swap_d.wait_recv()

    def stage_out(g):
        at = pl.ds(g * lanes, lanes)
        return pltpu.make_async_copy(stage.at[g % 2], og.at[:, :, :, at], local.at[4 + g % 2])

    for g in range(fs):
        at = slice(g * lanes, (g + 1) * lanes)
        part_sum = dot_tn(
            dsp[:, :, e_at(core)].reshape(2 * rows, he), a_pad[:, :, at].reshape(2 * rows, lanes)
        )
        part_sum = part_sum.astype(BF).reshape(nz, slot // grain, grain, lanes)
        if g >= 2:
            stage_out(g - 2).wait()
        stage[g % 2] = part_sum[:, : og.shape[1]]
        stage_out(g).start()
    for g in range(max(fs - 2, 0), fs):
        stage_out(g).wait()

    p_total.end()
    for h in range(2):
        p_sum[half_z(h)] = p_total.total(h).astype(BF)
    for i in range(1, cs):
        back = lax.rem(rank + cs - i, cs)
        to = d_att.at[pl.ds(pl.multiple_of(back * rows, rows), rows)]
        remote(to, to, d_send.at[0], d_recv.at[back], z=z).wait_recv()

    for i in range(1, nz):
        p2_copy(i).wait_send()
    for i in range(cs - 1):
        d_copy(i).wait_send()
    for g in range(fs):
        fc_pass(g).wait_send()
        p_pass(g).wait_send()
    fc_gather.sent()
    p_gather.sent()
    p_total.sent()
    keep_out.wait()
    h_line.finish()
    r_line.sent()
    for s in (swap_h2, swap_act, swap_db, swap_a, swap_d):
        s.wait_send()


def middle_part(cfg, a_own, tok, ct, ct_split, vec, fb, o_all, p1, fc):
    fs, nz, d, heads = cfg
    cs = 2 * nz
    rows, width = tok.shape[0], heads * HD
    length = rows * cs
    lanes = o_all.shape[3] // fs
    he, hf = ct_split.shape[1] // 2, fc.shape[2]
    share, grain = p1.shape[1], p1.shape[2]
    return pl.pallas_call(
        partial(middle_kernel, cfg),
        out_shape=(
            shape((rows, d), F32),
            shape((rows, d), F32),
            shape((length, width)),
            shape((nz, rows, 2 * he)),
            shape((d, hf)),
            shape((nz, share, grain, 2 * hf)),
            shape((nz,) + o_all.shape[1:]),
            shape((5, max(2 * hf, d)), F32),
        ),
        in_specs=[VMEM] * 6 + [HBM] * 3,
        out_specs=(VMEM, VMEM, VMEM, HBM, VMEM, VMEM, HBM, VMEM),
        scratch_shapes=[
            pltpu.VMEM((2, rows, fs * lanes), BF),
            pltpu.VMEM(o_all.shape, BF),
            pltpu.VMEM((fs * fc.shape[0], fc.shape[1], 2 * hf), BF),
            pltpu.VMEM((2, nz, fs, share, grain, 2 * hf), BF),
            pltpu.VMEM((nz, share, grain, 2 * hf), BF),
            pltpu.VMEM((nz, rows, 2 * he), BF),
            pltpu.VMEM((nz, rows, he), BF),
            pltpu.VMEM((2, nz, rows, d), BF),
            pltpu.VMEM((2, nz, rows, 2 * hf), BF),
            pltpu.VMEM((nz, rows, 2 * hf), BF),
            pltpu.VMEM((nz, rows, hf), BF),
            pltpu.VMEM((nz, rows, d), BF),
            pltpu.VMEM((nz, rows, d), BF),
            pltpu.VMEM((nz, rows, d), BF),
            pltpu.VMEM((rows, d), F32),
            pltpu.VMEM((rows, cs * width), BF),
            pltpu.VMEM((2, rows, 2 * he), BF),
            pltpu.VMEM((nz, fs, share, grain, 2 * hf), BF),
            pltpu.VMEM((2 * (fs - 1), nz - nz // 2, share, grain, 2 * hf), BF),
            pltpu.VMEM((2, nz) + o_all.shape[1:3] + (lanes,), BF),
        ]
        + sems(7, nz, nz, 2 * fs, (fs, 2), fs, fs, 2 * fs, (fs, 2), fs, fs)
        + sems(nz, nz, nz, nz, nz, nz, 6, 6, nz, nz, nz, cs, cs, 2 * fs, 2 * fs),
        name="middle",
        compiler_params=pltpu.CompilerParams(
            collective_id=1, has_side_effects=True, vmem_limit_bytes=62 * 2**20
        ),
    )(a_own, tok, ct, ct_split, vec, fb, o_all, p1, fc)


def last_kernel(
    cfg,
    qkv,
    att,
    lse,
    d_att,
    pos_col,
    pos_row,
    w,
    h1,
    tok,
    middle,
    d_middle,
    vec,
    sums,
    out_part,
    p_sum,
    og,
    output,
    input_grad,
    q_grad,
    p_grad,
    o_grad,
    small_grad,
    d_qkv,
    acc,
    h1v,
    qg,
    qr,
    qs,
    om,
    orc,
    osum,
    o_left,
    o_right,
    op,
    ro_left,
    ro_right,
    pz,
    other,
    partner,
    own,
    r_out,
    r_left,
    r_right,
    line,
    sm_out,
    sm_in,
    sm_f,
    ro_sems,
    ro_lsems,
    ro_rsems,
    z_send,
    z_recv,
    l_send,
    l_recv,
    local,
    q_send,
    q_recv,
    o_send,
    o_recv,
    os_send,
    os_left,
    os_right,
    m_send,
    m_recv,
    r_send,
    r_lsems,
    r_rsems,
    b_send,
    b_recv,
    s_send,
    s_recv,
    g_send,
    g_recv,
):
    fs, nz, d, heads = cfg
    cs = 2 * nz
    f, z, core = lax.axis_index("fsdp"), lax.axis_index("z"), lax.axis_index("core")
    rank = 2 * z + core
    rows = tok.shape[0]
    width = heads * HD
    lanes = w.shape[2] // fs
    grain = w.shape[1]
    own_rows, part = d // fs, d // cs
    he = out_part.shape[2] // 2
    slot = he // nz
    plane = Plane(fs)
    ranks = [lax.rem(rank + i, cs) for i in range(1, cs)]
    lanes_of = lambda g: pl.ds(pl.multiple_of(g * lanes, 128), lanes)
    runs = column_segments(cs, d, width, grain)
    block_rows = lambda b: pl.ds(pl.multiple_of(b * rows, rows), rows)
    half_z = lambda h: pl.ds(*halves(nz)[h])

    def h1_in(i):
        here = h1.at[:, lanes_of(lax.rem(f + 1 + i, fs))]
        return pltpu.make_async_copy(here, h1v.at[i % 2], local.at[4 + i % 2])

    for i in range(min(2, fs)):
        h1_in(i).start()
    om_in = pltpu.make_async_copy(og, om, local.at[2])
    op_in = pltpu.make_async_copy(out_part, op, local.at[3])
    om_in.start()
    op_in.start()
    meet(
        [dict(z=r // 2, core=lax.rem(r, 2)) for r in ranks] + [dict(fsdp=p) for p in plane.peers]
    )

    om_in.wait()
    o_total = PlaneSum(
        plane,
        lambda g, h: om.at[half_z(h), :, :, lanes_of(g)],
        lambda n, h: orc.at[n, pl.ds(0, halves(nz)[h][1])],
        (o_send, o_recv),
    )
    o_total.start()

    def z_copy(i):
        to = lax.rem(z + i, nz)
        return remote(p_sum.at[to], pz.at[z], z_send.at[to], z_recv.at[z], z=to)

    z_keep = pltpu.make_async_copy(p_sum.at[z], pz.at[z], local.at[0])
    for i in range(1, nz):
        z_copy(i).start()
    z_keep.start()

    op_in.wait()
    ro_line = LineSum(op, ro_left, ro_right, nz, (ro_sems, ro_lsems, ro_rsems))
    ro_line.first()

    def l_copy(i):
        g = plane.peers[i]
        return remote(pz.at[g], p_grad.at[f], l_send.at[i], l_recv.at[f], fsdp=g)

    l_keep = pltpu.make_async_copy(pz.at[f], p_grad.at[f], local.at[1])

    def shares_on():
        z_keep.wait()
        for i in range(1, nz):
            back = lax.rem(z + nz - i, nz)
            remote(pz.at[back], pz.at[back], z_send.at[0], z_recv.at[back], z=back).wait_recv()
        for i in range(fs - 1):
            l_copy(i).start()
        l_keep.start()

    tall = query_block(cs * rows)
    for h in range(heads):
        attend_back_head(
            h, width, tall, qkv, pos_col, pos_row, att, lse, d_att, d_qkv, acc
        )
        if h == heads - 1:
            ro_line.step(1)
            shares_on()

    slices = 3 * width // grain
    q_total = PlaneSum(
        plane,
        lambda g, h: qg.at[g, pl.ds(*halves(slices)[h])],
        lambda n, h: qr.at[n, pl.ds(0, halves(slices)[h][1])],
        (q_send, q_recv),
    )

    for i in range(fs):
        g = lax.rem(f + 1 + i, fs)
        h1_in(i).wait()
        part_sum = dot_tn(d_qkv[...], h1v[i % 2])
        qg[g] = part_sum.astype(BF).reshape(slices, grain, lanes)
        if i + 2 < fs:
            h1_in(i + 2).start()
    q_total.start()
    for s in range(2, nz - 1):
        ro_line.step(s)

    def hidden(block):
        full = dot(d_qkv[block_rows(block), :], w[...].reshape(3 * width, fs * lanes))
        return [full[:, lanes * g : lanes * g + own_rows] for g in range(fs)]

    def other_step(b, _):
        for g, piece in enumerate(hidden(2 * b + 1 - core)):
            other[b, :, own_rows * g : own_rows * (g + 1)] = piece.astype(BF)
        return 0

    lax.fori_loop(0, nz, other_step, 0)
    to_partner = remote(other, partner, m_send.at[0], m_recv.at[0], core=1 - core)
    to_partner.start()
    o_total.mid()

    to_partner.wait_recv()

    def own_step(i, _):
        b = lax.rem(z + 1 + i, nz)
        for g, piece in enumerate(hidden(2 * b + core)):
            at = slice(own_rows * g, own_rows * (g + 1))
            both = piece + partner[b, :, at].astype(F32)
            r_out[b, :, at] = both.astype(BF)

            @pl.when(b == z)
            def _():
                own[:, at] = both

        return 0

    lax.fori_loop(0, nz, own_step, 0)
    r_line = LineSum(r_out, r_left, r_right, nz, (r_send, r_lsems, r_rsems))
    r_line.first()
    q_total.mid()
    ro_line.finish()

    step = min(32, rows)

    def output_chunk(i, _):
        at = pl.ds(pl.multiple_of(i * step, step), step)
        total = (
            op[z, at, :].astype(F32)
            + ro_left[z, at, :].astype(F32)
            + ro_right[z, at, :].astype(F32)
        )
        for c in range(cs):
            low = (c % 2) * he + (c // 2) * slot
            cols = slice(c * part, (c + 1) * part)
            output[at, cols] = (
                middle[at, cols] + total[:, low : low + part] + vec[1:2, cols]
            ).astype(BF)
        return 0

    lax.fori_loop(0, rows // step, output_chunk, 0)
    o_total.end()
    for h in range(2):
        osum[half_z(h)] = o_total.total(h).astype(BF)
    o_line = LineSum(osum, o_left, o_right, nz, (os_send, os_left, os_right))
    o_line.first()
    r_line.step(1)

    q_total.end()
    for h in range(2):
        qs[pl.ds(*halves(slices)[h])] = q_total.total(h).astype(BF)

    def run_copy(n):
        dst, at, src, first, count = runs[n]
        here, there = qs.at[pl.ds(first, count)], q_grad.at[pl.ds(at, count)]
        if src == dst:
            return pltpu.make_async_copy(here, there, b_send.at[n])
        return remote(here, there, b_send.at[n], b_recv.at[n], z=dst // 2, core=dst % 2)

    for n, run in enumerate(runs):

        @pl.when(rank == run[2])
        def _():
            run_copy(n).start()

    for s in range(2, nz - 1):
        r_line.step(s)
    for s in range(1, nz - 1):
        o_line.step(s)
    r_line.finish()

    line[...] = jnp.zeros(line.shape, F32)

    def norm_back_chunk(i, _):
        at = pl.ds(pl.multiple_of(i * step, step), step)
        g = own[at, :] + r_left[z, at, :].astype(F32) + r_right[z, at, :].astype(F32)
        xhat, rstd = norm_rows(tok[at, :].astype(F32))
        input_grad[at, :] = d_middle[at, :] + norm_back(g, xhat, rstd, vec[0:1, :])
        line[0:1, 0:d] += jnp.sum(g * xhat, axis=0, keepdims=True)
        line[1:2, 0:d] += jnp.sum(g, axis=0, keepdims=True)
        return 0

    lax.fori_loop(0, rows // step, norm_back_chunk, 0)

    head_lanes = pl.ds(pl.multiple_of(rank * width, 128), width)
    line[2:3, head_lanes] = jnp.sum(d_qkv[:, 0:width].astype(F32), axis=0, keepdims=True)
    line[3:4, head_lanes] = jnp.sum(d_qkv[:, 2 * width :].astype(F32), axis=0, keepdims=True)
    line[4:8, 0:d] = sums[0:4, 0:d]
    sm_out[...] = jnp.zeros(sm_out.shape, F32)
    ff_parts = small_grad.shape[0] - 8
    hf = p_grad.shape[3] // 2
    for r in range(cs):
        sm_out[r, 0:8, 0:part] = line[0:8, r * part : (r + 1) * part]
    for k in range(2):
        for j in range(ff_parts):
            sm_out[2 * z + k, 8 + j : 9 + j, 0:part] = sums[
                4:5, k * hf + j * part : k * hf + (j + 1) * part
            ]

    def s_copy(i):
        r = ranks[i]
        here = sm_out.at[r]
        return remote(
            here, sm_in.at[rank], s_send.at[i], s_recv.at[rank], z=r // 2, core=lax.rem(r, 2)
        )

    for i in range(cs - 1):
        s_copy(i).start()
    o_line.finish()
    o_grad[...] = (
        osum[z].astype(F32) + o_left[z].astype(F32) + o_right[z].astype(F32)
    ).astype(o_grad.dtype)
    total = sm_out[rank]
    for i in range(1, cs):
        back = lax.rem(rank + cs - i, cs)
        remote(sm_in.at[back], sm_in.at[back], s_send.at[0], s_recv.at[back], z=z).wait_recv()
        total += sm_in[back]
    sm_f[f] = total

    def g_copy(i):
        return remote(sm_f.at[f], sm_f.at[f], g_send.at[i], g_recv.at[f], fsdp=plane.peers[i])

    for i in range(fs - 1):
        g_copy(i).start()
    for n, run in enumerate(runs):

        @pl.when(rank == run[0])
        def _():
            if run[0] == run[2]:
                run_copy(n).wait()
            else:
                run_copy(n).wait_recv()

    l_keep.wait()
    for g in plane.peers:
        remote(p_grad.at[g], p_grad.at[g], l_send.at[0], l_recv.at[g], fsdp=g).wait_recv()
    for g in plane.peers:
        remote(sm_f.at[g], sm_f.at[g], g_send.at[0], g_recv.at[g], fsdp=g).wait_recv()
    total = sm_f[0]
    for g in range(1, fs):
        total += sm_f[g]
    small_grad[...] = total

    for i in range(1, nz):
        z_copy(i).wait_send()
    for i in range(fs - 1):
        l_copy(i).wait_send()
        g_copy(i).wait_send()
    for s in (ro_line, r_line, o_line, o_total, q_total):
        s.sent()
    to_partner.wait_send()
    for n, run in enumerate(runs):
        if run[0] != run[2]:

            @pl.when(rank == run[2])
            def _():
                run_copy(n).wait_send()

    for i in range(cs - 1):
        s_copy(i).wait_send()


def last_part(cfg, counts, qkv, att, lse, d_att, pos, w, h1, tok, middle, d_middle, vec, sums, out_part, p_sum, og):
    fs, nz, d, heads = cfg
    cs = 2 * nz
    rows, length, width = tok.shape[0], qkv.shape[0], heads * HD
    grain, lanes = w.shape[1], w.shape[2] // fs
    q_grains, small_rows = counts
    he = out_part.shape[2] // 2
    slices = 3 * width // grain
    runs = len(column_segments(cs, d, width, grain))
    part = d // cs
    rest = 2 * (fs - 1)
    rows_low = pltpu.VMEM((nz, rows, d), BF)
    outs_low = pltpu.VMEM((nz, rows, 2 * he), BF)
    owner = (nz,) + og.shape[1:3] + (lanes,)
    return pl.pallas_call(
        partial(last_kernel, cfg),
        out_shape=(
            shape((rows, d)),
            shape((rows, d), F32),
            shape((q_grains, grain, lanes)),
            shape((fs,) + p_sum.shape[1:]),
            shape(owner[1:]),
            shape((small_rows, up(part)), F32),
        ),
        in_specs=[VMEM] * 7 + [HBM] + [VMEM] * 5 + [HBM, VMEM, HBM],
        out_specs=(VMEM,) * 6,
        scratch_shapes=[
            pltpu.VMEM((length, 3 * width), BF),
            pltpu.VMEM((length, 2 * HD), F32),
            pltpu.VMEM((2, length, lanes), BF),
            pltpu.VMEM((fs, slices, grain, lanes), BF),
            pltpu.VMEM((rest, slices - slices // 2, grain, lanes), BF),
            pltpu.VMEM((slices, grain, lanes), BF),
            pltpu.VMEM(og.shape, BF),
            pltpu.VMEM((rest, nz - nz // 2) + owner[1:], BF),
            pltpu.VMEM(owner, BF),
            pltpu.VMEM(owner, BF),
            pltpu.VMEM(owner, BF),
            outs_low,
            outs_low,
            outs_low,
            pltpu.VMEM(p_sum.shape, BF),
            rows_low,
            rows_low,
            pltpu.VMEM((rows, d), F32),
            rows_low,
            rows_low,
            rows_low,
            pltpu.VMEM((8, width * cs), F32),
            pltpu.VMEM((cs, small_rows, up(part)), F32),
            pltpu.VMEM((cs, small_rows, up(part)), F32),
            pltpu.VMEM((fs, small_rows, up(part)), F32),
        ]
        + sems(nz, nz, nz, nz, nz, fs, fs, 6, rest + 2, rest + 2, rest + 2, rest + 2)
        + sems(nz, nz, nz, 1, 1, nz, nz, nz, runs, runs, cs, cs, fs, fs),
        name="last",
        compiler_params=pltpu.CompilerParams(
            collective_id=2, has_side_effects=True, vmem_limit_bytes=62 * 2**20
        ),
    )(
        qkv,
        att,
        lse,
        d_att,
        pos[:, None],
        pos[None, :],
        w,
        h1,
        tok,
        middle,
        d_middle,
        vec,
        sums,
        out_part,
        p_sum,
        og,
    )


def body(
    tokens,
    block_order,
    cotangent,
    pre_attn_gain,
    pre_attn_bias,
    qkv_weight,
    query_bias,
    value_bias,
    out_weight,
    out_bias,
    pre_mlp_gain,
    pre_mlp_bias,
    fc_weight,
    fc_bias,
    proj_weight,
    proj_bias,
):
    fs, nz = lax.axis_size("fsdp"), lax.axis_size("z")
    cs = nz * 2
    rows, d = tokens.shape[1], tokens.shape[2]
    length = rows * cs
    heads_all = d // HD
    heads = -(-heads_all // cs)
    width = heads * HD
    part, own_rows = d // cs, d // fs
    fc_cols = fc_weight.shape[1]
    hf = up(fc_cols)

    small = jnp.stack(
        [
            pre_attn_gain,
            pre_attn_bias,
            query_bias,
            value_bias,
            out_bias,
            pre_mlp_gain,
            pre_mlp_bias,
            proj_bias,
        ]
    )
    small = jnp.concatenate([small, fc_bias.reshape(-1, part)]).astype(F32)
    small = jnp.pad(small, ((0, 0), (0, up(part) - part)))
    lanes = up(own_rows)
    wq = jnp.pad(qkv_weight.T, ((0, 0), (0, lanes - own_rows)))
    grain = math.gcd(math.gcd(wq.shape[0], HD), 8)
    wq = wq.reshape(-1, grain, lanes)
    fine = math.gcd(part, 8)
    share = -(-part // (fine * fs))
    slot = fs * share * fine
    he = nz * slot
    pj = proj_weight.T.reshape(part, 2, fc_cols)
    pj = jnp.pad(pj, ((0, slot - part), (0, 0), (0, hf - fc_cols)))
    pj = pj.reshape(fs * share, fine, 2 * hf)
    ot = jnp.pad(out_weight.T, ((0, 0), (0, lanes - own_rows))).reshape(-1, fine, lanes)
    pos = positions(block_order, length)
    fc = jnp.pad(fc_weight, ((0, 0), (0, hf - fc_cols)))
    fc = fc.reshape(-1, math.gcd(own_rows, 16), hf)
    cfg = (fs, nz, d, heads)
    h1, w, qkv, att, lse, smalls, p1, o_all, a_own = start(
        cfg, tokens[0], wq, small, pj, ot, pos
    )
    vec = lambda i: smalls[:, i, :part].reshape(d)
    gain1, pb = vec(0), vec(7)
    vecs = jnp.stack([vec(4), vec(5), vec(6)])
    fb = smalls[:, 8:, :part].reshape(cs, -1)
    fb = lax.dynamic_slice_in_dim(fb, lax.axis_index("z") * 2, 2, 0)
    fb = jnp.pad(fb, ((0, 0), (0, hf - fc_cols))).reshape(1, 2 * hf)

    ct_split = cotangent[0].reshape(rows, nz, 2, part).transpose(0, 2, 1, 3)
    ct_split = jnp.pad(ct_split, ((0, 0), (0, 0), (0, 0), (0, slot - part))).reshape(rows, 2 * he)
    middle, d_middle, d_att, out_part, fc_grad, p_sum, og, sums = middle_part(
        cfg, a_own, tokens[0], cotangent[0], ct_split, vecs, fb, o_all, p1, fc
    )
    fc_grad = lax.psum_scatter(fc_grad, "fsdp", scatter_dimension=0, tiled=True)
    fc_grad = lax.optimization_barrier(fc_grad)[:, :fc_cols]
    output, input_grad, q_grad, p_grad, out_grad, g = last_part(
        cfg,
        (wq.shape[0], small.shape[0]),
        qkv,
        att,
        lse,
        d_att,
        pos,
        w,
        h1,
        tokens[0],
        middle,
        d_middle,
        jnp.stack([gain1, pb]),
        sums,
        out_part,
        p_sum,
        og,
    )
    out_grad = out_grad.reshape(part, lanes)[:, :own_rows].T
    qkv_grad = q_grad.reshape(-1, lanes)[:, :own_rows].T
    proj_grad = p_grad.reshape(slot, 2, hf)[:part, :, :fc_cols].reshape(part, -1).T
    g = g[:, :part]
    return (
        output[None],
        input_grad[None],
        g[0],
        g[1],
        qkv_grad.astype(F32),
        g[2],
        g[3],
        out_grad.astype(F32),
        g[4],
        g[5],
        g[6],
        fc_grad.astype(F32),
        g[8:].reshape(-1),
        proj_grad.astype(F32),
        g[7],
    )


def solution(mesh):
    fs, cs = mesh.shape["fsdp"], mesh.shape["ctx"]
    split = Mesh(mesh.devices.reshape(fs, cs // 2, 2), ("fsdp", "z", "core"))
    rows = P("fsdp", CTX, None)
    weight = P("fsdp", CTX)
    vector = P(CTX)
    in_specs = (
        rows,
        P(),
        rows,
        vector,
        vector,
        weight,
        vector,
        vector,
        weight,
        vector,
        vector,
        vector,
        weight,
        vector,
        weight,
        vector,
    )
    out_specs = (
        rows,
        rows,
        vector,
        vector,
        weight,
        vector,
        vector,
        weight,
        vector,
        vector,
        vector,
        weight,
        vector,
        weight,
        vector,
    )
    return jax.shard_map(body, mesh=split, in_specs=in_specs, out_specs=out_specs, check_vma=False)
```

time: 1160 us -> 461 us (0.40)
  waiting for transfers between devices: 721 us -> 0.02 us
  Pallas kernels: 105 us -> 404 us
  local copies, waits for them, and re-layouts: 180 us -> 30.1 us
  matrix products: 65.6 us -> 0 us
  blocking collectives: 28.2 us -> 0 us
  other arithmetic: 29 us -> 7.24 us
    unnamed x27 -> x2, waiting for transfers between devices: 430 us -> 0.02 us
    pallas_call x2 -> x3, Pallas kernels: 105 us -> 404 us  [the longest x1 155 us: middle_part(): pl.pallas_call(partial(middle_kernel, cfg), out_shape=(shape((rows, d), F...]
    all_gather x8 -> x0, waiting for transfers between devices: 173 us -> none  [the longest x1 42.4 us: body(): h2 = lax.all_gather(h2_own, 'z', axis=0, tiled=True)]
    reduce_scatter x5 -> x0, waiting for transfers between devices: 103 us -> none  [the longest x1 38.1 us: body(): lax.psum_scatter(qkv_grad, 'fsdp', scatter_dimension=0, tiled=True)]
    dot_general x11 -> x0, matrix products: 65.6 us -> none  [the longest x4 26 us: dot(): return jnp.dot(a, b, preferred_element_type=F32)]
    unnamed x85 -> x27, local copies, waits for them, and re-layouts: 72.4 us -> 9.73 us
    dynamic_update_slice x4 -> x0, local copies, waits for them, and re-layouts: 48.2 us -> none  [the longest x1 47.6 us: body(): lax.dynamic_update_slice_in_dim(full, proj_grad, lax.axis_index('z') * ff...]
    all_to_all x1 -> x0, blocking collectives: 18.1 us -> none  [body(): lax.all_to_all(d_att_own, CTX, split_axis=1, concat_axis=0, tiled=True)]
  transfers between devices with their start and end apart: 21 -> 1, of which waited for: 18 -> 0; matrix products, arithmetic and copies ran while one was open for 19% -> 2% of each run, Pallas kernels for 8% -> 31%
where the time goes in v2:
time: 461 us; the launch traced here: 456 us
  Pallas kernels  404 us (88%)
  local copies, waits for them, and re-layouts  30.1 us (7%)
  between operations  14.5 us (3%)
  other arithmetic  7.24 us (2%)
    pallas_call x1, Pallas kernels, middle_part(): pl.pallas_call(partial(middle_kernel, cfg), out_shape=(shape((rows, d), F...  155 us
    pallas_call x1, Pallas kernels, last_part(): pl.pallas_call(partial(last_kernel, cfg), out_shape=(shape((rows, d)), sh...  140 us
    pallas_call x1, Pallas kernels, start(): pl.pallas_call(partial(start_kernel, cfg), out_shape=(shape((length, fs *...  109 us
    unnamed x27, local copies, waits for them, and re-layouts  9.73 us
  transfers between devices with their start and end apart: 1, of which 0 were waited for; matrix products, arithmetic and copies ran while one was open for 2% of the time, Pallas kernels for 31%

profile of v2, /device:TPU:0, one launch (start us, length us, event | category | flops | bytes accessed | tf_op | source)
XLA Modules:
  0.0 455.8 jit_solution(4265378112910383583)
XLA Ops:
  7.2 0.7 broadcast_multiply_fusion
  8.0 0.7 add.56.pos_row
  8.7 1.3 add.60.pos_col
  10.6 0.7 stack.31
  11.3 0.7 stack.32
  11.9 0.7 stack.33
  12.6 0.7 stack.34
  13.2 0.7 stack.35
  13.9 0.7 stack.36
  14.6 0.7 stack.37
  15.2 0.8 reshape.119
  16.7 1.0 copy.78
  17.7 0.7 pad_bitcast_fusion.1.ot
  18.4 2.0 copy.63
  20.6 0.9 pad_bitcast_fusion.wq
  21.5 0.7 reshape.120
  22.9 1.4 reshape.121.pj
  24.3 108.9 %start.1 = (bf16[1024,2048]{1,0:T(8,128)(2,1)}, bf16[96,8,2048]{2,1,0:T(8,128)(2,1)}, bf16[1024,768]{1,0:T(8,128)(2,1)}, bf16[1024,256]{1,0:T(8,128)(2,1)}, f32[...) custom-call(bf16[128,1600]{1,0:T(8,128)(2,1)} %bitcast.40, ...), custom_call_target="tpu_custom_call" | custom-call | tf_op jit(solution)/shard_map/start/pallas_call | solution.py:654
  133.2 0.9 slice.70
  134.1 1.1 slice_reduce_fusion.1
  135.3 1.0 copy.67
  136.3 1.0 copy.69.ct_split
  137.3 0.9 pad.37
  139.9 155.4 %middle.1 = (f32[128,1600]{1,0:T(8,128)}, f32[128,1600]{1,0:T(8,128)}, bf16[1024,256]{1,0:T(8,128)(2,1)}, bf16[4,128,1792]{2,1,0:T(8,128)(2,1)}, bf16[1600,896]{...) custom-call(bf16[128,2048]{1,0:T(8,128)(2,1)} %get-tuple-element.41.a_own, ...), custom_call_target="tpu_custom_call" | custom-call | tf_op jit(solution)/shard_map/middle/pallas_call | solution.py:1060
  296.1 139.7 %last.1 = (bf16[128,1600]{1,0:T(8,128)(2,1)}, f32[128,1600]{1,0:T(8,128)}, bf16[75,8,512]{2,1,0:T(8,128)(2,1)}, bf16[4,7,8,1792]{3,2,1,0:T(8,128)(2,1)}, bf16[25,8,512]{2,1,0:T(8,128)(2,1)}, /*index=5*/f32[12,256]{1,0:T(8,128)}) custom-call(bf16[1024,768]{1,0:T(8,128)(2,1)} %get-tuple-element.38.qkv, bf16[1024,256]{1,0:T(8,128)(2,1)} %get-tuple-element.39.att, ...), custom_call_target="tpu_custom_call" | custom-call | tf_op jit(solution)/shard_map/last/pallas_call | solution.py:1466
  435.8 2.1 copy.73
  437.9 2.3 copy.74
  440.2 0.7 reshape.129
  442.0 2.0 reshape.131
  444.6 0.8 convert_bitcast_fusion.1
  445.4 1.0 convert_bitcast_fusion
  446.4 2.3 slice_convert_fusion.1
  (44 shorter events, 6.5 us)
Async XLA Ops:
  7.2 13.2 %copy-start.5 = (bf16[400,600]{1,0:T(8,128)(2,1)S(1)}, bf16[400,600]{1,0:T(8,128)(2,1)}, u32[]{:S(2)}) copy-start(bf16[400,600]{1,0:T(8,128)(2,1)} %param.21) | copy-start | bytes 1440004
  7.2 439.2 %reduce-scatter.4.cloned.1.call-start = ((), (), s32[]{:S(2)}) async-start(), calls=%async_computation.1 | async-start | bytes 3584000
  17.7 3.8 copy-start.3
  22.9 112.4 %copy-start = (bf16[1,128,1600]{1,2,0:T(8,128)(2,1)S(1)}, bf16[1,128,1600]{1,2,0:T(8,128)(2,1)}, u32[]{:S(2)}) copy-start(bf16[1,128,1600]{1,2,0:T(8,128)(2,1)} %param.18) | copy-start | bytes 1228804
  133.2 4.1 copy-start.2
  435.7 4.4 copy-start.7
  435.8 5.1 %copy-start.6 = (bf16[25,8,512]{2,1,0:T(8,128)(2,1)S(1)}, bf16[25,8,512]{2,1,0:T(8,128)(2,1)}, u32[]{:S(2)}) copy-start(bf16[25,8,512]{2,1,0:T(8,128)(2,1)} %get-tuple-element.58) | copy-start | bytes 614404
  435.8 5.2 %copy-start.4 = (bf16[75,8,512]{2,1,0:T(8,128)(2,1)S(1)}, bf16[75,8,512]{2,1,0:T(8,128)(2,1)}, u32[]{:S(2)}) copy-start(bf16[75,8,512]{2,1,0:T(8,128)(2,1)} %get-tuple-element.57) | copy-start | bytes 1843204
  435.8 5.5 %copy-start.1 = (bf16[4,7,8,1792]{3,2,1,0:T(8,128)(2,1)S(1)}, bf16[4,7,8,1792]{3,2,1,0:T(8,128)(2,1)}, u32[]{:S(2)}) copy-start(bf16[4,7,8,1792]{3,2,1,0:T(8,128)(2,1)} %get-tuple-element.60) | copy-start | bytes 2408452
Sparse Core Ops, SparseCore 0:
  295.4 71.2 reduce-scatter.3

commit v3 on v2

--- a/solution.py
+++ b/solution.py
@@ -173,6 +173,22 @@
         return remote(
             self.parts.at[block], there, self.send.at[block], recv.at[block], z=self.z + way
         )
+
+    def order(self, i):
+        near = self.z < self.size // 2
+        ahead = self.size - 1 - self.z
+        from_low = jnp.where(i < ahead, self.size - 1 - i, i - ahead)
+        from_high = jnp.where(i < self.z, i, self.size - 1 - (i - self.z))
+        return jnp.where(near, from_low, from_high)
+
+    def ready(self, block):
+        @pl.when((self.z == 0) & (block > 0))
+        def _():
+            self.copy(block, 1).start()
+
+        @pl.when((self.z == self.size - 1) & (block < self.size - 1))
+        def _():
+            self.copy(block, -1).start()
 
     def first(self):
         for way, edge in ((1, 0), (-1, self.size - 1)):
@@ -408,11 +424,12 @@
     att,
     lse,
     smalls,
-    p1,
+    p2,
     o_all,
     a_own,
     toks,
     vecs,
+    p1,
     small_send,
     small_recv,
     q_send,
@@ -427,6 +444,8 @@
     c_recv,
     p1_send,
     p1_recv,
+    p2_send,
+    p2_recv,
     p_local,
     a_send,
     a_recv,
@@ -453,8 +472,8 @@
     planes = plane.peers
 
     w[:, :, lanes_of(f)] = jnp.zeros((w.shape[0], grain, lanes), BF)
-    own_out = o_all.at[rank, :, :, lanes_of(f)]
-    pltpu.sync_copy(ot, own_out)
+    keep_out = pltpu.make_async_copy(ot, o_all.at[rank, :, :, lanes_of(f)], p_local.at[0])
+    keep_out.start()
     ranks = [lax.rem(rank + i, cs) for i in range(1, cs)]
     meet([dict(z=r // 2, core=lax.rem(r, 2)) for r in ranks] + [dict(fsdp=p) for p in planes])
 
@@ -485,33 +504,34 @@
         here = pj.at[pl.ds(planes[i] * share, share)]
         return remote(here, p1.at[f], p1_send.at[i], p1_recv.at[f], fsdp=planes[i])
 
-    p1_local = pltpu.make_async_copy(pj.at[pl.ds(f * share, share)], p1.at[f], p_local.at[0])
-    p1_local.start()
+    p1[f] = pj[pl.ds(f * share, share)]
     for i in range(fs - 1):
         p1_copy(i).start()
 
-    def ox_copy(i, block):
+    def ox_copy(i, block, here=None):
         at = o_all.at[2 * block + core, :, :, lanes_of(f)]
-        return remote(at, at, ox_send.at[i, block], ox_recv.at[f, block], fsdp=planes[i])
+        here = at if here is None else here
+        return remote(here, at, ox_send.at[i, block], ox_recv.at[f, block], fsdp=planes[i])
 
     def ox_arrival(g, block):
         at = o_all.at[2 * block + core, :, :, lanes_of(g)]
         return remote(at, at, ox_send.at[0, block], ox_recv.at[g, block], fsdp=g)
 
-    def oc_copy(g, block):
+    def oc_copy(g, block, here=None):
         at = o_all.at[2 * block + core, :, :, lanes_of(g)]
-        return remote(at, at, oc_send.at[g, block], oc_recv.at[g, block], core=1 - core)
+        here = at if here is None else here
+        return remote(here, at, oc_send.at[g, block], oc_recv.at[g, block], core=1 - core)
 
     def oc_arrival(g, block):
         at = o_all.at[2 * block + 1 - core, :, :, lanes_of(g)]
         return remote(at, at, oc_send.at[g, block], oc_recv.at[g, block], core=1 - core)
 
-    def out_block(block):
+    def out_block(block, here=None):
         for i in range(fs - 1):
-            ox_copy(i, block).start()
-        oc_copy(f, block).start()
-
-    out_block(z)
+            ox_copy(i, block, here).start()
+        oc_copy(f, block, here).start()
+
+    out_block(z, ot)
 
     for n, run in enumerate(runs):
 
@@ -555,12 +575,25 @@
 
     for s in range(1, nz):
         line.step(s, lambda b: pass_on(b).start())
+        if s == 1:
+            gather.mid()
 
     out_line = Line(
         lambda b: o_all.at[2 * b + core, :, :, lanes_of(f)], nz, (o_right, o_left, o_recv)
     )
+    keep_out.wait()
     out_line.start()
-    gather.mid()
+
+    for g in planes:
+        remote(p1.at[g], p1.at[g], p1_send.at[0], p1_recv.at[g], fsdp=g).wait_recv()
+
+    def p2_copy(i):
+        to = lax.rem(z + i, nz)
+        return remote(p1.at[to], p2.at[z], p2_send.at[to], p2_recv.at[z], z=to)
+
+    for i in range(1, nz):
+        p2_copy(i).start()
+    p2[z] = p1[z]
     for b in range(nz):
         arrival(b).wait_recv()
 
@@ -614,9 +647,9 @@
         back = lax.rem(rank + cs - i, cs)
         to = a_own.at[:, pl.ds(pl.multiple_of(back * width, 128), width)]
         remote(to, to, a_send.at[0], a_recv.at[back], z=z).wait_recv()
-    p1_local.wait()
-    for g in planes:
-        remote(p1.at[g], p1.at[g], p1_send.at[0], p1_recv.at[g], fsdp=g).wait_recv()
+    for i in range(1, nz):
+        back = lax.rem(z + nz - i, nz)
+        remote(p2.at[back], p2.at[back], p2_send.at[0], p2_recv.at[back], z=back).wait_recv()
     for g in range(fs):
         for b in range(nz):
             oc_arrival(g, b).wait_recv()
@@ -632,6 +665,8 @@
         small_copy(i).wait_send()
         a_copy(i).wait_send()
     gather.sent()
+    for i in range(1, nz):
+        p2_copy(i).wait_send()
     for i in range(fs - 1):
         p1_copy(i).wait_send()
         for b in range(nz):
@@ -660,17 +695,19 @@
             shape((length, width)),
             shape((heads, length), F32),
             shape((cs,) + small.shape, F32),
-            shape((fs, pj.shape[0] // fs) + pj.shape[1:]),
+            shape((nz, pj.shape[0] // fs) + pj.shape[1:]),
             shape((cs,) + ot.shape[:2] + (fs * lanes,)),
             shape((rows, cs * width)),
         ),
-        in_specs=[VMEM, VMEM, VMEM, HBM, HBM, VMEM, VMEM],
-        out_specs=(VMEM, VMEM, VMEM, VMEM, VMEM, VMEM, HBM, HBM, VMEM),
+        in_specs=[VMEM] * 7,
+        out_specs=(VMEM,) * 7 + (HBM, VMEM),
         scratch_shapes=[
             pltpu.VMEM((cs, rows, d), BF),
             pltpu.VMEM((8, width * cs), F32),
+            pltpu.VMEM((fs, pj.shape[0] // fs) + pj.shape[1:], BF),
         ]
-        + sems(cs, cs, runs, runs, runs, 2 * fs, (fs, 2), nz, nz, nz, nz, nz, fs, fs, 1, cs, cs)
+        + sems(cs, cs, runs, runs, runs, 2 * fs, (fs, 2), nz, nz, nz, nz, nz)
+        + sems(fs, fs, nz, nz, 1, cs, cs)
         + sems(nz, nz, nz, (fs, nz), (fs, nz), (fs, nz), (fs, nz)),
         name="start",
         compiler_params=pltpu.CompilerParams(
@@ -684,11 +721,9 @@
     a_own,
     tok,
     ct,
-    ct_split,
-    vec,
-    fb,
+    smalls,
+    p2,
     o_all,
-    p1,
     fc,
     middle,
     d_middle,
@@ -698,11 +733,12 @@
     p_sum,
     og,
     sums,
+    vec,
+    fb,
     a_pad,
     ov,
     fcv,
     pjv,
-    p2,
     ctb,
     cto,
     h2b,
@@ -719,8 +755,6 @@
     pr,
     stage,
     local,
-    p2_send,
-    p2_recv,
     p3_send,
     p3_recv,
     pc_send,
@@ -753,9 +787,9 @@
     width = heads * HD
     lanes = o_all.shape[3] // fs
     own_rows, part = d // fs, d // cs
-    share, grain = p1.shape[1], p1.shape[2]
-    he, hf = ct_split.shape[1] // 2, fc.shape[2]
-    slot = he // nz
+    share, grain = p2.shape[1], p2.shape[2]
+    slot = fs * share * grain
+    he, hf = nz * slot, fc.shape[2]
     ff = 2 * hf
     fc_rows = fc.shape[0]
     tall = nz * rows
@@ -773,11 +807,9 @@
         pltpu.make_async_copy(fc.at[pl.ds(*halves(fc_rows)[h])], fc_at(f, core, h), local.at[1 + h])
         for h in range(2)
     ]
-    load_p2 = pltpu.make_async_copy(p1.at[z], p2.at[z], local.at[3])
     load_out.start()
     for copy in load_fc:
         copy.start()
-    load_p2.start()
     meet(
         [dict(z=r // 2, core=lax.rem(r, 2)) for r in ranks] + [dict(fsdp=p) for p in plane.peers]
     )
@@ -785,12 +817,20 @@
     def swap(n, here, there):
         return remote(here, there, e_send.at[n], e_recv.at[n], core=1 - core)
 
-    def p2_copy(i):
-        to = lax.rem(z + i, nz)
-        return remote(p1.at[to], p2.at[z], p2_send.at[to], p2_recv.at[z], z=to)
-
-    for i in range(1, nz):
-        p2_copy(i).start()
+    half_z = lambda h: pl.ds(*halves(nz)[h])
+    pjv[core, :, f] = p2[...]
+    p_gather = PlaneGather(plane, lambda g, h: pjv.at[core, half_z(h), g], (p3_send, p3_recv))
+    p_gather.start()
+
+    def p_pass(g):
+        at = pjv.at[core, :, g]
+        return remote(at, at, pc_send.at[g], pc_recv.at[g], core=1 - core)
+
+    def p_came(g):
+        at = pjv.at[1 - core, :, g]
+        return remote(at, at, pc_send.at[g], pc_recv.at[g], core=1 - core)
+
+    p_pass(f).start()
 
     for copy in load_fc:
         copy.wait()
@@ -807,9 +847,20 @@
 
     fc_pass(f).start()
 
-    ctb[z] = ct_split[...]
+    ctb[z] = jnp.zeros(ctb.shape[1:], BF)
+    for c in range(cs):
+        to = (c % 2) * he + (c // 2) * slot
+        ctb[z, :, to : to + part] = ct[:, c * part : (c + 1) * part]
     c_line = Line(lambda b: ctb.at[b], nz, (c_right, c_left, c_recv))
     c_line.start()
+
+    for r in range(cs):
+        vec[:, r * part : (r + 1) * part] = smalls[r, 4:7, 0:part]
+    fb[...] = jnp.zeros(fb.shape, F32)
+    for k in range(2):
+        for j in range(smalls.shape[1] - 8):
+            to = k * hf + j * part
+            fb[:, to : to + part] = smalls[2 * z + k, 8 + j : 9 + j, 0:part]
 
     for g in range(fs):
         a_pad[core, :, lanes * g : lanes * g + own_rows] = a_own[
@@ -833,80 +884,78 @@
     lax.fori_loop(0, rows // step, norm_chunk, 0)
     h_line = Line(lambda b: h2b.at[core, b], nz, (h_right, h_left, h_recv))
     h_line.start()
+    p_gather.mid()
     c_line.step(1)
+    h_line.step(1)
     fc_gather.mid()
-    h_line.step(1)
-
-    load_p2.wait()
-    for i in range(1, nz):
-        back = lax.rem(z + nz - i, nz)
-        remote(p2.at[back], p2.at[back], p2_send.at[0], p2_recv.at[back], z=back).wait_recv()
-    half_z = lambda h: pl.ds(*halves(nz)[h])
-    pjv[core, :, f] = p2[...]
-    p_gather = PlaneGather(plane, lambda g, h: pjv.at[core, half_z(h), g], (p3_send, p3_recv))
-    p_gather.start()
-
-    def p_pass(g):
-        at = pjv.at[core, :, g]
-        return remote(at, at, pc_send.at[g], pc_recv.at[g], core=1 - core)
-
-    def p_came(g):
-        at = pjv.at[1 - core, :, g]
-        return remote(at, at, pc_send.at[g], pc_recv.at[g], core=1 - core)
-
-    p_pass(f).start()
-    for s in range(2, nz):
+    for s in range(2, nz - 1):
         c_line.step(s)
         h_line.step(s)
+    p_gather.end()
+    for g in plane.peers:
+        p_pass(g).start()
+    fc_gather.end()
+    for g in plane.peers:
+        fc_pass(g).start()
+    for g in range(fs):
+        p_came(g).wait_recv()
+    for g in range(fs):
+        fc_came(g).wait_recv()
+
+    chunk = 256 if ff % 256 == 0 else 128
+    some = nz // 2
+    wide = some * rows
+    sums[4:5, :] = jnp.zeros((1, sums.shape[1]), F32)
+
+    def feed(first, i):
+        at = pl.ds(pl.multiple_of(i * chunk, chunk), chunk)
+        blocks = pl.ds(first, some)
+        w = fcv[:, :, at].reshape(d, chunk)
+        before = dot(h2b[core, blocks].reshape(wide, d), w) + fb[:, at]
+        act, slope = gelu_pair(before)
+        actb[core, blocks, :, at] = act.astype(BF).reshape(some, rows, chunk)
+        w = pjv[:, :, :, :, :, at].reshape(2 * he, chunk)
+        back = dot(ctb[blocks].reshape(wide, 2 * he), w)
+        low = (back * slope).astype(BF)
+        dbo[blocks, :, at] = low.reshape(some, rows, chunk)
+        sums[4:5, at] += jnp.sum(low.astype(F32), axis=0, keepdims=True)
+
+    def feed_half(first):
+        def one(i, _):
+            feed(first, i)
+            return 0
+
+        lax.fori_loop(0, ff // chunk, one, 0)
+
+    near = z // some * some
+    feed_half(near)
+    c_line.step(nz - 1)
+    h_line.step(nz - 1)
     swap_ct = swap(0, ctb.at[:, :, e_at(1 - core)], cto)
     swap_h2 = swap(1, h2b.at[core], h2b.at[core])
     swap_h2.start()
     swap_ct.start()
-    fc_gather.end()
-    for g in plane.peers:
-        fc_pass(g).start()
-    p_gather.mid()
-    for g in range(fs):
-        fc_came(g).wait_recv()
-    p_gather.end()
-    for g in plane.peers:
-        p_pass(g).start()
-    for g in range(fs):
-        p_came(g).wait_recv()
-
-    chunk = 256 if ff % 256 == 0 else 128
-
-    def feed(i, _):
-        at = pl.ds(pl.multiple_of(i * chunk, chunk), chunk)
-        before = dot(h2b[core].reshape(tall, d), fcv[:, :, at].reshape(d, chunk)) + fb[:, at]
-        act, slope = gelu_pair(before)
-        actb[core, :, :, at] = act.astype(BF).reshape(nz, rows, chunk)
-        back = dot(ctb[...].reshape(tall, 2 * he), pjv[:, :, :, :, :, at].reshape(2 * he, chunk))
-        low = (back * slope).astype(BF)
-        dbo[:, :, at] = low.reshape(nz, rows, chunk)
-        sums[4:5, at] = jnp.sum(low.astype(F32), axis=0, keepdims=True)
-        return 0
-
-    lax.fori_loop(0, ff // chunk, feed, 0)
+    feed_half(some - near)
     swap_act = swap(2, actb.at[core], actb.at[core])
     swap_db = swap(3, dbo.at[:, :, half_at(1 - core)], dbp)
     swap_act.start()
     swap_db.start()
 
+    r_line = LineSum(dh, in_left, in_right, nz, (r_send, r_left, r_right))
+
     def hidden_back(i, _):
-        block = lax.rem(z + 1 + i, nz)
-        part = dot_nt(dbo[block], fcv[...].reshape(d, ff))
-        dh[block] = part.astype(BF)
+        block = r_line.order(i)
+        part_sum = dot_nt(dbo[block], fcv[...].reshape(d, ff))
+        dh[block] = part_sum.astype(BF)
 
         @pl.when(block == z)
         def _():
-            own_dh[...] = part
-
+            own_dh[...] = part_sum
+
+        r_line.ready(block)
         return 0
 
     lax.fori_loop(0, nz, hidden_back, 0)
-    r_line = LineSum(dh, in_left, in_right, nz, (r_send, r_left, r_right))
-    r_line.first()
 
     def output_part(k, i):
         w = pjv[k, i].reshape(slot, ff)
@@ -1032,8 +1081,6 @@
         to = d_att.at[pl.ds(pl.multiple_of(back * rows, rows), rows)]
         remote(to, to, d_send.at[0], d_recv.at[back], z=z).wait_recv()
 
-    for i in range(1, nz):
-        p2_copy(i).wait_send()
     for i in range(cs - 1):
         d_copy(i).wait_send()
     for g in range(fs):
@@ -1049,14 +1096,14 @@
         s.wait_send()
 
 
-def middle_part(cfg, a_own, tok, ct, ct_split, vec, fb, o_all, p1, fc):
+def middle_part(cfg, a_own, tok, ct, smalls, p2, o_all, fc):
     fs, nz, d, heads = cfg
     cs = 2 * nz
     rows, width = tok.shape[0], heads * HD
     length = rows * cs
     lanes = o_all.shape[3] // fs
-    he, hf = ct_split.shape[1] // 2, fc.shape[2]
-    share, grain = p1.shape[1], p1.shape[2]
+    share, grain = p2.shape[1], p2.shape[2]
+    he, hf = nz * fs * share * grain, fc.shape[2]
     return pl.pallas_call(
         partial(middle_kernel, cfg),
         out_shape=(
@@ -1069,14 +1116,15 @@
             shape((nz,) + o_all.shape[1:]),
             shape((5, max(2 * hf, d)), F32),
         ),
-        in_specs=[VMEM] * 6 + [HBM] * 3,
+        in_specs=[VMEM] * 5 + [HBM] * 2,
         out_specs=(VMEM, VMEM, VMEM, HBM, VMEM, VMEM, HBM, VMEM),
         scratch_shapes=[
+            pltpu.VMEM((3, d), F32),
+            pltpu.VMEM((1, 2 * hf), F32),
             pltpu.VMEM((2, rows, fs * lanes), BF),
             pltpu.VMEM(o_all.shape, BF),
             pltpu.VMEM((fs * fc.shape[0], fc.shape[1], 2 * hf), BF),
             pltpu.VMEM((2, nz, fs, share, grain, 2 * hf), BF),
-            pltpu.VMEM((nz, share, grain, 2 * hf), BF),
             pltpu.VMEM((nz, rows, 2 * he), BF),
             pltpu.VMEM((nz, rows, he), BF),
             pltpu.VMEM((2, nz, rows, d), BF),
@@ -1093,13 +1141,13 @@
             pltpu.VMEM((2 * (fs - 1), nz - nz // 2, share, grain, 2 * hf), BF),
             pltpu.VMEM((2, nz) + o_all.shape[1:3] + (lanes,), BF),
         ]
-        + sems(7, nz, nz, 2 * fs, (fs, 2), fs, fs, 2 * fs, (fs, 2), fs, fs)
+        + sems(7, 2 * fs, (fs, 2), fs, fs, 2 * fs, (fs, 2), fs, fs)
         + sems(nz, nz, nz, nz, nz, nz, 6, 6, nz, nz, nz, cs, cs, 2 * fs, 2 * fs),
         name="middle",
         compiler_params=pltpu.CompilerParams(
             collective_id=1, has_side_effects=True, vmem_limit_bytes=62 * 2**20
         ),
-    )(a_own, tok, ct, ct_split, vec, fb, o_all, p1, fc)
+    )(a_own, tok, ct, smalls, p2, o_all, fc)
 
 
 def last_kernel(
@@ -1113,19 +1161,24 @@
     w,
     h1,
     tok,
-    middle,
-    d_middle,
-    vec,
+    smalls,
     sums,
     out_part,
     p_sum,
     og,
-    output,
-    input_grad,
+    fg,
+    out_rows,
+    in_rows,
     q_grad,
     p_grad,
     o_grad,
+    f_grad,
     small_grad,
+    vec,
+    p_all,
+    q_own,
+    fgv,
+    fr,
     d_qkv,
     acc,
     h1v,
@@ -1166,6 +1219,8 @@
     os_send,
     os_left,
     os_right,
+    f_send,
+    f_recv,
     m_send,
     m_recv,
     r_send,
@@ -1189,6 +1244,7 @@
     own_rows, part = d // fs, d // cs
     he = out_part.shape[2] // 2
     slot = he // nz
+    hf = p_sum.shape[3] // 2
     plane = Plane(fs)
     ranks = [lax.rem(rank + i, cs) for i in range(1, cs)]
     lanes_of = lambda g: pl.ds(pl.multiple_of(g * lanes, 128), lanes)
@@ -1206,6 +1262,10 @@
     op_in = pltpu.make_async_copy(out_part, op, local.at[3])
     om_in.start()
     op_in.start()
+    fg_in = pltpu.make_async_copy(fg, fgv, local.at[6])
+    fg_in.start()
+    for r in range(cs):
+        vec[:, r * part : (r + 1) * part] = smalls[r, 0:1, 0:part]
     meet(
         [dict(z=r // 2, core=lax.rem(r, 2)) for r in ranks] + [dict(fsdp=p) for p in plane.peers]
     )
@@ -1234,9 +1294,9 @@
 
     def l_copy(i):
         g = plane.peers[i]
-        return remote(pz.at[g], p_grad.at[f], l_send.at[i], l_recv.at[f], fsdp=g)
-
-    l_keep = pltpu.make_async_copy(pz.at[f], p_grad.at[f], local.at[1])
+        return remote(pz.at[g], p_all.at[f], l_send.at[i], l_recv.at[f], fsdp=g)
+
+    l_keep = pltpu.make_async_copy(pz.at[f], p_all.at[f], local.at[1])
 
     def shares_on():
         z_keep.wait()
@@ -1272,6 +1332,14 @@
         if i + 2 < fs:
             h1_in(i + 2).start()
     q_total.start()
+    fg_in.wait()
+    f_rows = f_grad.shape[0]
+    f_total = PlaneSum(
+        plane,
+        lambda g, h: fgv.at[pl.ds(g * f_rows + halves(f_rows)[h][0], halves(f_rows)[h][1])],
+        lambda n, h: fr.at[n, pl.ds(0, halves(f_rows)[h][1])],
+        (f_send, f_recv),
+    )
     for s in range(2, nz - 1):
         ro_line.step(s)
 
@@ -1291,8 +1359,10 @@
 
     to_partner.wait_recv()
 
+    r_line = LineSum(r_out, r_left, r_right, nz, (r_send, r_lsems, r_rsems))
+
     def own_step(i, _):
-        b = lax.rem(z + 1 + i, nz)
+        b = r_line.order(i)
         for g, piece in enumerate(hidden(2 * b + core)):
             at = slice(own_rows * g, own_rows * (g + 1))
             both = piece + partner[b, :, at].astype(F32)
@@ -1302,12 +1372,12 @@
             def _():
                 own[:, at] = both
 
+        r_line.ready(b)
         return 0
 
     lax.fori_loop(0, nz, own_step, 0)
-    r_line = LineSum(r_out, r_left, r_right, nz, (r_send, r_lsems, r_rsems))
-    r_line.first()
     q_total.mid()
+    f_total.start()
     ro_line.finish()
 
     step = min(32, rows)
@@ -1322,9 +1392,7 @@
         for c in range(cs):
             low = (c % 2) * he + (c // 2) * slot
             cols = slice(c * part, (c + 1) * part)
-            output[at, cols] = (
-                middle[at, cols] + total[:, low : low + part] + vec[1:2, cols]
-            ).astype(BF)
+            out_rows[at, cols] = total[:, low : low + part]
         return 0
 
     lax.fori_loop(0, rows // step, output_chunk, 0)
@@ -1341,7 +1409,7 @@
 
     def run_copy(n):
         dst, at, src, first, count = runs[n]
-        here, there = qs.at[pl.ds(first, count)], q_grad.at[pl.ds(at, count)]
+        here, there = qs.at[pl.ds(first, count)], q_own.at[pl.ds(at, count)]
         if src == dst:
             return pltpu.make_async_copy(here, there, b_send.at[n])
         return remote(here, there, b_send.at[n], b_recv.at[n], z=dst // 2, core=dst % 2)
@@ -1356,6 +1424,16 @@
         r_line.step(s)
     for s in range(1, nz - 1):
         o_line.step(s)
+    f_total.mid()
+
+    l_keep.wait()
+    for g in plane.peers:
+        remote(p_all.at[g], p_all.at[g], l_send.at[0], l_recv.at[g], fsdp=g).wait_recv()
+    fine = p_all.shape[2]
+    whole = p_all[...].reshape(-1, fine, 2 * hf)[: part // fine].reshape(part, 2 * hf)
+    ff_half = p_grad.shape[0] // 2
+    for k in range(2):
+        p_grad[k * ff_half : (k + 1) * ff_half, :] = whole[:, k * hf : k * hf + ff_half].T
     r_line.finish()
 
     line[...] = jnp.zeros(line.shape, F32)
@@ -1364,7 +1442,7 @@
         at = pl.ds(pl.multiple_of(i * step, step), step)
         g = own[at, :] + r_left[z, at, :].astype(F32) + r_right[z, at, :].astype(F32)
         xhat, rstd = norm_rows(tok[at, :].astype(F32))
-        input_grad[at, :] = d_middle[at, :] + norm_back(g, xhat, rstd, vec[0:1, :])
+        in_rows[at, :] = norm_back(g, xhat, rstd, vec[...])
         line[0:1, 0:d] += jnp.sum(g * xhat, axis=0, keepdims=True)
         line[1:2, 0:d] += jnp.sum(g, axis=0, keepdims=True)
         return 0
@@ -1377,7 +1455,6 @@
     line[4:8, 0:d] = sums[0:4, 0:d]
     sm_out[...] = jnp.zeros(sm_out.shape, F32)
     ff_parts = small_grad.shape[0] - 8
-    hf = p_grad.shape[3] // 2
     for r in range(cs):
         sm_out[r, 0:8, 0:part] = line[0:8, r * part : (r + 1) * part]
     for k in range(2):
@@ -1396,9 +1473,8 @@
     for i in range(cs - 1):
         s_copy(i).start()
     o_line.finish()
-    o_grad[...] = (
-        osum[z].astype(F32) + o_left[z].astype(F32) + o_right[z].astype(F32)
-    ).astype(o_grad.dtype)
+    whole = (osum[z].astype(F32) + o_left[z].astype(F32) + o_right[z].astype(F32)).astype(BF)
+    o_grad[...] = whole.reshape(part, lanes)[:, :own_rows].T
     total = sm_out[rank]
     for i in range(1, cs):
         back = lax.rem(rank + cs - i, cs)
@@ -1420,9 +1496,10 @@
             else:
                 run_copy(n).wait_recv()
 
-    l_keep.wait()
-    for g in plane.peers:
-        remote(p_grad.at[g], p_grad.at[g], l_send.at[0], l_recv.at[g], fsdp=g).wait_recv()
+    q_grad[...] = q_own[...].reshape(-1, lanes)[:, :own_rows].T
+    f_total.end()
+    for h in range(2):
+        f_grad[pl.ds(*halves(f_rows)[h])] = f_total.total(h).astype(BF)
     for g in plane.peers:
         remote(sm_f.at[g], sm_f.at[g], g_send.at[0], g_recv.at[g], fsdp=g).wait_recv()
     total = sm_f[0]
@@ -1435,7 +1512,7 @@
     for i in range(fs - 1):
         l_copy(i).wait_send()
         g_copy(i).wait_send()
-    for s in (ro_line, r_line, o_line, o_total, q_total):
+    for s in (ro_line, r_line, o_line, o_total, q_total, f_total):
         s.sent()
     to_partner.wait_send()
     for n, run in enumerate(runs):
@@ -1449,12 +1526,14 @@
         s_copy(i).wait_send()
 
 
-def last_part(cfg, counts, qkv, att, lse, d_att, pos, w, h1, tok, middle, d_middle, vec, sums, out_part, p_sum, og):
+def last_part(cfg, counts, qkv, att, lse, d_att, pos, w, h1, tok, smalls, sums, out_part, p_sum, og, fg):
     fs, nz, d, heads = cfg
     cs = 2 * nz
     rows, length, width = tok.shape[0], qkv.shape[0], heads * HD
     grain, lanes = w.shape[1], w.shape[2] // fs
-    q_grains, small_rows = counts
+    q_grains, fc_cols = counts
+    small_rows = smalls.shape[1]
+    f_rows = fg.shape[0] // fs
     he = out_part.shape[2] // 2
     slices = 3 * width // grain
     runs = len(column_segments(cs, d, width, grain))
@@ -1466,16 +1545,22 @@
     return pl.pallas_call(
         partial(last_kernel, cfg),
         out_shape=(
-            shape((rows, d)),
             shape((rows, d), F32),
-            shape((q_grains, grain, lanes)),
-            shape((fs,) + p_sum.shape[1:]),
-            shape(owner[1:]),
+            shape((rows, d), F32),
+            shape((d // fs, q_grains * grain)),
+            shape((2 * fc_cols, part)),
+            shape((d // fs, part)),
+            shape((f_rows,) + fg.shape[1:]),
             shape((small_rows, up(part)), F32),
         ),
-        in_specs=[VMEM] * 7 + [HBM] + [VMEM] * 5 + [HBM, VMEM, HBM],
-        out_specs=(VMEM,) * 6,
+        in_specs=[VMEM] * 7 + [HBM] + [VMEM] * 3 + [HBM, VMEM, HBM, HBM],
+        out_specs=(VMEM,) * 7,
         scratch_shapes=[
+            pltpu.VMEM((1, d), F32),
+            pltpu.VMEM((fs,) + p_sum.shape[1:], BF),
+            pltpu.VMEM((q_grains, grain, lanes), BF),
+            pltpu.VMEM(fg.shape, BF),
+            pltpu.VMEM((rest, f_rows - f_rows // 2) + fg.shape[1:], BF),
             pltpu.VMEM((length, 3 * width), BF),
             pltpu.VMEM((length, 2 * HD), F32),
             pltpu.VMEM((2, length, lanes), BF),
@@ -1502,8 +1587,8 @@
             pltpu.VMEM((cs, small_rows, up(part)), F32),
             pltpu.VMEM((fs, small_rows, up(part)), F32),
         ]
-        + sems(nz, nz, nz, nz, nz, fs, fs, 6, rest + 2, rest + 2, rest + 2, rest + 2)
-        + sems(nz, nz, nz, 1, 1, nz, nz, nz, runs, runs, cs, cs, fs, fs),
+        + sems(nz, nz, nz, nz, nz, fs, fs, 7, rest + 2, rest + 2, rest + 2, rest + 2)
+        + sems(nz, nz, nz, rest + 2, rest + 2, 1, 1, nz, nz, nz, runs, runs, cs, cs, fs, fs),
         name="last",
         compiler_params=pltpu.CompilerParams(
             collective_id=2, has_side_effects=True, vmem_limit_bytes=62 * 2**20
@@ -1518,13 +1603,12 @@
         w,
         h1,
         tok,
-        middle,
-        d_middle,
-        vec,
+        smalls,
         sums,
         out_part,
         p_sum,
         og,
+        fg,
     )
 
 
@@ -1559,17 +1643,20 @@
 
     small = jnp.stack(
         [
-            pre_attn_gain,
-            pre_attn_bias,
-            query_bias,
-            value_bias,
-            out_bias,
-            pre_mlp_gain,
-            pre_mlp_bias,
-            proj_bias,
+            v.astype(F32)
+            for v in (
+                pre_attn_gain,
+                pre_attn_bias,
+                query_bias,
+                value_bias,
+                out_bias,
+                pre_mlp_gain,
+                pre_mlp_bias,
+                proj_bias,
+            )
         ]
     )
-    small = jnp.concatenate([small, fc_bias.reshape(-1, part)]).astype(F32)
+    small = jnp.concatenate([small, fc_bias.astype(F32).reshape(-1, part)])
     small = jnp.pad(small, ((0, 0), (0, up(part) - part)))
     lanes = up(own_rows)
     wq = jnp.pad(qkv_weight.T, ((0, 0), (0, lanes - own_rows)))
@@ -1579,34 +1666,26 @@
     share = -(-part // (fine * fs))
     slot = fs * share * fine
     he = nz * slot
-    pj = proj_weight.T.reshape(part, 2, fc_cols)
-    pj = jnp.pad(pj, ((0, slot - part), (0, 0), (0, hf - fc_cols)))
-    pj = pj.reshape(fs * share, fine, 2 * hf)
+    pj = jnp.pad(
+        proj_weight.reshape(2, fc_cols, part), ((0, 0), (0, hf - fc_cols), (0, slot - part))
+    )
+    pj = pj.reshape(2 * hf, slot).T.reshape(fs * share, fine, 2 * hf)
     ot = jnp.pad(out_weight.T, ((0, 0), (0, lanes - own_rows))).reshape(-1, fine, lanes)
     pos = positions(block_order, length)
     fc = jnp.pad(fc_weight, ((0, 0), (0, hf - fc_cols)))
     fc = fc.reshape(-1, math.gcd(own_rows, 16), hf)
     cfg = (fs, nz, d, heads)
-    h1, w, qkv, att, lse, smalls, p1, o_all, a_own = start(
+    h1, w, qkv, att, lse, smalls, p2, o_all, a_own = start(
         cfg, tokens[0], wq, small, pj, ot, pos
     )
     vec = lambda i: smalls[:, i, :part].reshape(d)
-    gain1, pb = vec(0), vec(7)
-    vecs = jnp.stack([vec(4), vec(5), vec(6)])
-    fb = smalls[:, 8:, :part].reshape(cs, -1)
-    fb = lax.dynamic_slice_in_dim(fb, lax.axis_index("z") * 2, 2, 0)
-    fb = jnp.pad(fb, ((0, 0), (0, hf - fc_cols))).reshape(1, 2 * hf)
-
-    ct_split = cotangent[0].reshape(rows, nz, 2, part).transpose(0, 2, 1, 3)
-    ct_split = jnp.pad(ct_split, ((0, 0), (0, 0), (0, 0), (0, slot - part))).reshape(rows, 2 * he)
     middle, d_middle, d_att, out_part, fc_grad, p_sum, og, sums = middle_part(
-        cfg, a_own, tokens[0], cotangent[0], ct_split, vecs, fb, o_all, p1, fc
-    )
-    fc_grad = lax.psum_scatter(fc_grad, "fsdp", scatter_dimension=0, tiled=True)
-    fc_grad = lax.optimization_barrier(fc_grad)[:, :fc_cols]
-    output, input_grad, q_grad, p_grad, out_grad, g = last_part(
+        cfg, a_own, tokens[0], cotangent[0], smalls, p2, o_all, fc
+    )
+    fg = fc_grad.reshape(-1, fc.shape[1], hf)
+    out_rows, in_rows, qkv_grad, proj_grad, out_grad, fc_grad, g = last_part(
         cfg,
-        (wq.shape[0], small.shape[0]),
+        (wq.shape[0], fc_cols),
         qkv,
         att,
         lse,
@@ -1615,17 +1694,16 @@
         w,
         h1,
         tokens[0],
-        middle,
-        d_middle,
-        jnp.stack([gain1, pb]),
+        smalls,
         sums,
         out_part,
         p_sum,
         og,
-    )
-    out_grad = out_grad.reshape(part, lanes)[:, :own_rows].T
-    qkv_grad = q_grad.reshape(-1, lanes)[:, :own_rows].T
-    proj_grad = p_grad.reshape(slot, 2, hf)[:part, :, :fc_cols].reshape(part, -1).T
+        fg,
+    )
+    output = (middle + out_rows + vec(7)).astype(BF)
+    input_grad = d_middle + in_rows
+    fc_grad = fc_grad.reshape(own_rows, hf)[:, :fc_cols]
     g = g[:, :part]
     return (
         output[None],

time: 461 us -> 387 us (0.84)
  Pallas kernels: 404 us -> 358 us
  between operations: 14.5 us -> 1.21 us
  local copies, waits for them, and re-layouts: 30.1 us -> 17.6 us
    pallas_call x1, Pallas kernels: 155 us -> 117 us  [middle_part(): pl.pallas_call(partial(middle_kernel, cfg), out_shape=(shape((rows, d), F...]
    pallas_call x1, Pallas kernels: 140 us -> 128 us  [last_part(): pl.pallas_call(partial(last_kernel, cfg), out_shape=(shape((rows, d), F32...]
    another operation x13 -> x8, local copies, waits for them, and re-layouts: 5.72 us -> 0.04 us  [body(): jnp.stack([v.astype(F32) for v in (pre_attn_gain, pre_attn_bias, query_bi...]
    unnamed x27 -> x48, local copies, waits for them, and re-layouts: 9.73 us -> 7.86 us
  transfers between devices with their start and end apart: 1 -> 0, of which waited for: 0 -> 0; matrix products, arithmetic and copies ran while one was open for 2% -> 0% of each run, Pallas kernels for 31% -> 0%
where the time goes in v3:
time: 387 us; the launch traced here: 383 us
  Pallas kernels  358 us (93%)
  local copies, waits for them, and re-layouts  17.6 us (5%)
  other arithmetic  5.92 us (2%)
    pallas_call x1, Pallas kernels, last_part(): pl.pallas_call(partial(last_kernel, cfg), out_shape=(shape((rows, d), F32...  128 us
    pallas_call x1, Pallas kernels, middle_part(): pl.pallas_call(partial(middle_kernel, cfg), out_shape=(shape((rows, d), F...  117 us
    pallas_call x1, Pallas kernels, start(): pl.pallas_call(partial(start_kernel, cfg), out_shape=(shape((length, fs *...  112 us
    unnamed x48, local copies, waits for them, and re-layouts  7.86 us

profile of v3, /device:TPU:0, one launch (start us, length us, event | category | flops | bytes accessed | tf_op | source)
XLA Modules:
  0.0 382.6 jit_solution(1750517564219390370)
XLA Ops:
  0.6 0.7 broadcast_multiply_fusion
  1.3 0.1 iota_add_fusion
  1.4 1.3 add.69.pos_col
  2.6 2.0 copy.38
  4.6 0.7 add.63.pos_row
  5.3 2.3 reshape.110
  7.6 0.0 copy-start.11
  7.6 0.0 copy-start.12
  7.7 0.6 pad.25
  8.3 1.0 copy.49
  9.3 0.2 copy.47
  9.6 0.9 pad_bitcast_fusion.wq
  10.5 0.1 copy.48
  10.6 0.7 pad_bitcast_fusion.1.ot
  11.3 0.1 reshape.109
  11.6 0.6 pad_convert_fusion.small
  12.2 112.0 %start.1 = (bf16[1024,2048]{1,0:T(8,128)(2,1)}, bf16[96,8,2048]{2,1,0:T(8,128)(2,1)}, bf16[1024,768]{1,0:T(8,128)(2,1)}, bf16[1024,256]{1,0:T(8,128)(2,1)}, f32[...) custom-call(bf16[128,1600]{1,0:T(8,128)(2,1)} %bitcast.33, ...), custom_call_target="tpu_custom_call" | custom-call | tf_op jit(solution)/shard_map/start/pallas_call | solution.py:689
  124.3 0.9 pad.27
  125.2 1.0 copy.42
  126.2 117.5 %middle.1 = (f32[128,1600]{1,0:T(8,128)}, f32[128,1600]{1,0:T(8,128)}, bf16[1024,256]{1,0:T(8,128)(2,1)}, bf16[4,128,1792]{2,1,0:T(8,128)(2,1)}, bf16[1600,896]{...) custom-call(bf16[128,2048]{1,0:T(8,128)(2,1)} %get-tuple-element.39.a_own, ...), custom_call_target="tpu_custom_call" | custom-call | tf_op jit(solution)/shard_map/middle/pallas_call | solution.py:1107
  243.6 128.3 %last.1 = (f32[128,1600]{1,0:T(8,128)}, f32[128,1600]{1,0:T(8,128)}, bf16[400,600]{1,0:T(8,128)(2,1)}, bf16[1600,200]{1,0:T(8,128)(2,1)}, bf16[400,200]{1,0:T(8,...) custom-call(bf16[1024,768]{1,0:T(8,128)(2,1)} %get-tuple-element.44.qkv, ...), custom_call_target="tpu_custom_call" | custom-call | tf_op jit(solution)/shard_map/last/pallas_call | solution.py:1545
  372.0 0.9 slice_reduce_fusion
  372.9 0.1 add.65
  373.0 1.6 add_bitcast_fusion
  374.6 1.2 copy.45
  375.7 0.9 copy.44
  376.7 1.2 slice_convert_fusion
  377.9 1.4 copy.46
  379.3 1.0 convert_element_type.21
  380.3 0.8 convert_element_type.22
  381.1 0.6 fusion.1
  381.7 0.7 reshape.117
  (48 shorter events, 0.2 us)
Async XLA Ops:
  1.4 8.0 %copy-start.6 = (bf16[400,600]{1,0:T(8,128)(2,1)S(1)}, bf16[400,600]{1,0:T(8,128)(2,1)}, u32[]{:S(2)}) copy-start(bf16[400,600]{1,0:T(8,128)(2,1)} %param.21) | copy-start | bytes 1440004
  7.6 2.9 copy-start.8
  7.6 3.7 copy-start.11
  7.6 3.8 copy-start.12
  7.6 3.8 copy-start.13
  7.7 3.8 copy-start.14
  7.7 3.8 copy-start.15
  7.7 3.8 copy-start.16
  7.7 3.8 copy-start.17
  7.7 3.8 %copy-start.18 = (bf16[200]{0:T(256)(128)(2,1)S(1)}, bf16[200]{0:T(256)(128)(2,1)}, u32[]{:S(2)}) copy-start(bf16[200]{0:T(256)(128)(2,1)} %param.27) | copy-start | bytes 1204
  7.7 3.8 %copy-start.19 = (bf16[200]{0:T(256)(128)(2,1)S(1)}, bf16[200]{0:T(256)(128)(2,1)}, u32[]{:S(2)}) copy-start(bf16[200]{0:T(256)(128)(2,1)} %param.31) | copy-start | bytes 1204
  9.3 114.9 %copy-start.4 = (bf16[400,800]{1,0:T(8,128)(2,1)S(1)}, bf16[400,800]{1,0:T(8,128)(2,1)}, u32[]{:S(2)}) copy-start(bf16[400,800]{1,0:T(8,128)(2,1)} %param.28) | copy-start | bytes 1920004
  9.6 115.6 %copy-start.7 = (bf16[1,128,1600]{1,2,0:T(8,128)(2,1)S(1)}, bf16[1,128,1600]{1,2,0:T(8,128)(2,1)}, u32[]{:S(2)}) copy-start(bf16[1,128,1600]{1,2,0:T(8,128)(2,1)} %param.18) | copy-start | bytes 1228804
  243.6 129.3 %copy-start = (f32[128,1600]{1,0:T(8,128)S(1)}, f32[128,1600]{1,0:T(8,128)}, u32[]{:S(2)}) copy-start(f32[128,1600]{1,0:T(8,128)} %get-tuple-element.43) | copy-start | bytes 2457604
  243.6 129.3 %copy-start.1 = (f32[128,1600]{1,0:T(8,128)S(1)}, f32[128,1600]{1,0:T(8,128)}, u32[]{:S(2)}) copy-start(f32[128,1600]{1,0:T(8,128)} %get-tuple-element.56) | copy-start | bytes 2457604
  374.5 2.1 copy-start.3
  374.6 3.3 copy-start.2
  375.7 3.5 copy-start.5
  376.7 3.6 copy-start.9
  376.7 4.4 %copy-start.10 = (f32[12,256]{1,0:T(8,128)S(1)}, f32[12,256]{1,0:T(8,128)}, u32[]{:S(2)}) copy-start(f32[12,256]{1,0:T(8,128)} %get-tuple-element.58) | copy-start | bytes 36868
